TPU v7x, 512 devices: a whole 4x4x16 slice. The times are simulated.
512 devices in a mesh: pair: 2 (over core), dp: 16 (over x, z_lo), fsdp: 16 (over y, z_hi).
Axes of the slice: x: 4, y: 4, z: 16 (z_hi: 4, z_lo: 4; z = z_hi * 4 + z_lo), core: 2. Of those that a mesh axis runs over, the one named last changes fastest.
Arguments:
- features: bfloat16 [2, 320, 262144], P('pair', None, ('dp', 'fsdp')), may hold values from -6 to 6
- level_gain: float32 [64, 320], replicated, may hold values from 0.5 to 1.5
- levels: int32 [64], replicated, may hold values from 0 to 63
- w_in: bfloat16 [2, 1280, 320], P('pair', 'fsdp'), may hold values from -0.3125 to 0.3125
- w_down: bfloat16 [2, 1280, 320], P('pair', 'fsdp'), may hold values from -0.15625 to 0.15625
- w_rgb: float32 [2, 3, 320], P('pair'), may hold values from -0.3125 to 0.3125
- target: float32 [3, 262144], P(None, ('dp', 'fsdp')), may hold values from -6 to 6
- counts: int32 [262144], P(('dp', 'fsdp')), may hold values from 1 to 1024
Outputs:
- predictions: float32 [2, 3, 262144], P('pair', None, ('dp', 'fsdp'))
- grad_in: float32 [2, 1280, 320], P('pair', 'fsdp')
- grad_down: float32 [2, 1280, 320], P('pair', 'fsdp')
All inputs are finite; a program needn't handle non-finite values.
Results may differ from a plain program's by a relative error of at most 0.0022.
Values may be sent and summed in bfloat16 or wider, within the bound.
A program may use at most 64 MiB of HBM per device.

v0:
```python
import math

import jax
import jax.numpy as jnp
from jax import lax
from jax.sharding import PartitionSpec as P

IMG_PIX = 4096


EPS = 1e-06
DISTILL = 1.0


def from_partner(value, axis, apart):
    return lax.ppermute(value, axis, [(i, i ^ 1 << apart) for i in range(lax.axis_size(axis))])


def contract_rows(left, right):
    return lax.dot_general(
        left, right, (((1,), (1,)), ((), ())), preferred_element_type=jnp.float32
    )


def on_device(features, level_gain, levels, w_in, w_down, w_rgb, target, counts):
    x_local = features[0]
    pixels = x_local.shape[1]
    offset = lax.axis_index(("dp", "fsdp")) * pixels
    image = offset // IMG_PIX
    level = jnp.sum(jnp.where(jnp.arange(levels.shape[0], dtype=jnp.int32) == image, levels, 0))
    table_rows = jnp.arange(level_gain.shape[0], dtype=jnp.int32)[:, None]
    gain = jnp.sum(jnp.where(table_rows == level, level_gain, 0.0), axis=0)
    xf = x_local.astype(jnp.float32)
    mean_sq = jnp.mean(xf * xf, axis=0, keepdims=True)
    normed = (xf * lax.rsqrt(mean_sq + EPS) * gain[:, None]).astype(jnp.bfloat16)
    pre = jnp.dot(
        lax.all_gather(w_in[0], "fsdp", axis=0, tiled=True),
        normed,
        preferred_element_type=jnp.float32,
    )
    hidden = jax.nn.silu(pre).astype(jnp.bfloat16)
    delta = lax.dot_general(
        lax.all_gather(w_down[0], "fsdp", axis=0, tiled=True),
        hidden,
        (((0,), (0,)), ((), ())),
        preferred_element_type=jnp.float32,
    )
    mixed = xf + delta
    pred = jnp.dot(w_rgb[0], mixed, precision=lax.Precision.HIGHEST)
    partner = from_partner(pred, "pair", 0)
    pixels_all = pixels * lax.axis_size("dp") * lax.axis_size("fsdp")
    loss_scale = math.sqrt(xf.shape[0] / pixels_all)
    samples = counts.astype(jnp.float32)
    weight = samples / (samples + 64.0)
    g_pred = (weight * (pred - target) + DISTILL * (pred - partner)) * loss_scale
    g_mixed = jnp.dot(w_rgb[0].T, g_pred, precision=lax.Precision.HIGHEST).astype(jnp.bfloat16)
    g_hidden = jnp.dot(
        lax.all_gather(w_down[0], "fsdp", axis=0, tiled=True),
        g_mixed,
        preferred_element_type=jnp.float32,
    )
    sig = jax.nn.sigmoid(pre)
    g_pre = (g_hidden * sig * (1.0 + pre * (1.0 - sig))).astype(jnp.bfloat16)
    channels = normed.shape[0]
    partial_rows = lax.psum_scatter(
        jnp.concatenate([contract_rows(g_pre, normed), contract_rows(hidden, g_mixed)], axis=1),
        "fsdp",
        scatter_dimension=0,
        tiled=True,
    )
    totals = lax.psum(partial_rows, "dp")
    return (pred[None], totals[:, :channels][None], totals[:, channels:][None])


def solution(mesh):
    in_specs = (
        P("pair", None, ("dp", "fsdp")),
        P(),
        P(),
        P("pair", "fsdp", None),
        P("pair", "fsdp", None),
        P("pair", None, None),
        P(None, ("dp", "fsdp")),
        P(("dp", "fsdp")),
    )
    out_specs = (P("pair", None, ("dp", "fsdp")), P("pair", "fsdp", None), P("pair", "fsdp", None))
    return jax.shard_map(
        on_device, mesh=mesh, in_specs=in_specs, out_specs=out_specs, check_vma=False
    )
```

profile of v0, /device:TPU:1, one launch (start us, length us, event | category | flops | bytes accessed | tf_op | source)
XLA Modules:
  0.0 495.5 jit_solution(17658378001316559053)
XLA Ops:
  7.2 0.0 copy-start
  7.2 0.0 copy-start.1
  7.2 0.0 reduce-scatter.4.cloned.1.call-start
  7.2 1.4 fusion.30
  8.6 0.6 iota_compare_fusion
  9.3 1.2 fusion.8
  10.5 67.9 %all-gather.1 = bf16[1,1280,320]{2,1,0:T(8,128)(2,1)S(1)} all-gather(bf16[1,80,320]{2,1,0:T(8,128)(2,1)} %param.12), channel_id=3, replica_groups=mesh['pair'=2,'dp'=16,'fsdp'=16] {'fsdp'}, dimensions={1}, use_global_device_ids=true | all-gather | bytes 870400 | tf_op jit(solution)/shard_map/all_gather | solution.py:43
  78.4 65.0 %all-gather = bf16[1,1280,320]{2,1,0:T(8,128)(2,1)S(1)} all-gather(bf16[1,80,320]{2,1,0:T(8,128)(2,1)} %param.11), channel_id=2, replica_groups=mesh['pair'=2,'dp'=16,'fsdp'=16] {'fsdp'}, dimensions={1}, use_global_device_ids=true | all-gather | bytes 870400 | tf_op jit(solution)/shard_map/all_gather | solution.py:37
  143.4 0.0 copy-done.1
  143.4 0.1 select_reduce_fusion
  143.5 0.0 copy-done
  143.5 4.3 fusion.5
  147.8 0.0 copy-start.2
  147.8 0.0 copy-start.4
  147.8 0.0 copy-start.3
  147.9 1.1 convert_add_fusion
  148.9 0.0 copy-done.2
  148.9 0.8 fusion.26
  149.7 16.3 %collective-permute-start = (f32[3,1024]{1,0:T(4,128)S(1)}, f32[3,1024]{1,0:T(4,128)S(1)}, u32[]{:S(2)}, u32[]{:S(2)}) collective-permute-start(f32[3,1024]{1,0:T(4,128)S(1)} %bitcast.76), channel_id=1, source_target_pairs={{0,256},{256,0},{1,257},{257,1},{2,258},{258,2},{3,259},{259,3},{4... | collective-permute-start | bytes 36872 | tf_op jit(solution)/shard_map/ppermute | solution.py:16
  166.1 0.0 copy-done.4
  166.1 0.8 collective-permute-done
  166.9 0.0 copy-done.3
  166.9 1.2 convolution_convert_fusion
  168.1 2.3 fusion.34
  170.4 6.5 %fusion.7 = f32[1280,320]{0,1:T(8,128)} fusion(f32[1024,1280]{1,0:T(8,128)} %get-tuple-element.12, bf16[1024,320]{0,1:T(8,128)(2,1)S(1)} %convolution_convert_fusion, bf16[1,1280,320]{2,1,0:T(8,128)(2,1)S(1)} %all-gather.1, bf16[1,320,1024]{2,1,0:T(8,128)(2,1)S(1)} %copy-done, f32[320]{0:T(512)S(1)} %select_reduce_fusion, f32[1024]{0:T(1024)S(1)} %add_rsqrt_fusion), kind=kOutput, calls=%fused_computation.16 | convolution fusion | flops 1690828800 | bytes 9016576 | tf_op jit(solution)/shard_map/dot_general | solution.py:20
  176.9 2.1 pad_maximum_fusion
  179.1 3.1 copy.17
  182.2 0.0 reduce-scatter.4.cloned.1.call-update
  182.2 0.0 all-reduce.2.cloned.1.call-start
  182.3 147.8 %reduce-scatter.4.cloned.1.call-done = f32[80,640]{1,0:T(8,128)} async-done(((f32[1280,640]{1,0:T(8,128)}), f32[80,640]{1,0:T(8,128)}) %reduce-scatter.4.cloned.1.call-update) | async-done | bytes 204816
  330.1 1.8 copy.18
  331.9 0.0 all-reduce.2.cloned.1.call-update
  331.9 0.6 copy.14
  332.5 153.6 %all-reduce.2.cloned.1.call-done = f32[80,640]{0,1:T(8,128)} async-done(((f32[80,640]{0,1:T(8,128)}), f32[80,640]{0,1:T(8,128)}) %all-reduce.2.cloned.1.call-update) | async-done | bytes 204816 | tf_op jit(solution)/shard_map/psum | solution.py:71
  486.1 1.0 slice_bitcast_fusion
  487.1 0.8 copy.16
  487.9 0.8 copy.15
  (2 shorter events, 0.0 us)
Async XLA Ops:
  7.2 136.3 %copy-start = (bf16[1,320,1024]{2,1,0:T(8,128)(2,1)S(1)}, bf16[1,320,1024]{2,1,0:T(8,128)(2,1)}, u32[]{:S(2)}) copy-start(bf16[1,320,1024]{2,1,0:T(8,128)(2,1)} %param.8) | copy-start | bytes 1966084
  7.2 136.2 %copy-start.1 = (f32[64,320]{1,0:T(8,128)S(1)}, f32[64,320]{1,0:T(8,128)}, u32[]{:S(2)}) copy-start(f32[64,320]{1,0:T(8,128)} %param.9) | copy-start | bytes 245764
  7.2 322.9 %reduce-scatter.4.cloned.1.call-start = ((), (), s32[]{:S(2)}) async-start(), calls=%async_computation.2 | async-start | bytes 3481600
  147.8 1.1 copy-start.2
  147.8 18.2 %copy-start.4 = (s32[1024]{0:T(1024)S(1)}, s32[1024]{0:T(1024)}, u32[]{:S(2)}) copy-start(s32[1024]{0:T(1024)} %param.15) | copy-start | bytes 12292
  147.8 19.0 %copy-start.3 = (f32[3,1024]{1,0:T(4,128)S(1)}, f32[3,1024]{1,0:T(4,128)}, u32[]{:S(2)}) copy-start(f32[3,1024]{1,0:T(4,128)} %param.14) | copy-start | bytes 36868
  149.7 17.2 %collective-permute-start = (f32[3,1024]{1,0:T(4,128)S(1)}, f32[3,1024]{1,0:T(4,128)S(1)}, u32[]{:S(2)}, u32[]{:S(2)}) collective-permute-start(f32[3,1024]{1,0:T(4,128)S(1)} %bitcast.76), channel_id=1, source_target_pairs={{0,256},{256,0},{1,257},{257,1},{2,258},{258,2},{3,259},{259,3},{4... | collective-permute-start | bytes 36872 | tf_op jit(solution)/shard_map/ppermute | solution.py:16
  182.2 303.9 %all-reduce.2.cloned.1.call-start = ((), (), s32[]{:S(2)}) async-start(), calls=%async_computation.1 | async-start | bytes 655360 | tf_op jit(solution)/shard_map/psum | solution.py:71
Sparse Core Ops, SparseCore 0:
  182.4 147.6 reduce-scatter.3
  333.0 153.0 all-reduce.1
where the time goes:
time: 506 us; the launch traced here: 496 us
  waiting for transfers between devices  302 us (60%)
  blocking collectives  133 us (26%)
  starting transfers between devices  16.4 us (3%)
  matrix products  16.2 us (3%)
  between operations  14.1 us (3%)
  local copies, waits for them, and re-layouts  8.15 us (2%)
  other arithmetic  5.48 us (1%)
    psum x1, waiting for transfers between devices, on_device(): totals = lax.psum(partial_rows, 'dp')  154 us
    unnamed x3, waiting for transfers between devices  148 us
    all_gather x1, blocking collectives, on_device(): lax.all_gather(w_down[0], 'fsdp', axis=0, tiled=True)  67.9 us
    all_gather x1, blocking collectives, on_device(): lax.all_gather(w_in[0], 'fsdp', axis=0, tiled=True)  65 us
    ppermute x1, starting transfers between devices, from_partner(): lax.ppermute(value, axis, [(i, i ^ 1 << apart) for i in range(lax.axis_si...  16.3 us
  transfers between devices with their start and end apart: 3, of which 3 were waited for; matrix products, arithmetic and copies ran while one was open for 0% of the time, Pallas kernels for 0%

commit v1 on v0

--- a/solution.py
+++ b/solution.py
@@ -33,43 +33,42 @@
     xf = x_local.astype(jnp.float32)
     mean_sq = jnp.mean(xf * xf, axis=0, keepdims=True)
     normed = (xf * lax.rsqrt(mean_sq + EPS) * gain[:, None]).astype(jnp.bfloat16)
+    high = lax.Precision.HIGHEST
+    head_rows = lax.dot_general(
+        w_down[0].astype(jnp.float32), w_rgb[0], (((1,), (1,)), ((), ())), precision=high
+    )
+    head = lax.all_gather(head_rows, "fsdp", axis=0, tiled=True)
     pre = jnp.dot(
         lax.all_gather(w_in[0], "fsdp", axis=0, tiled=True),
         normed,
         preferred_element_type=jnp.float32,
     )
-    hidden = jax.nn.silu(pre).astype(jnp.bfloat16)
-    delta = lax.dot_general(
-        lax.all_gather(w_down[0], "fsdp", axis=0, tiled=True),
-        hidden,
-        (((0,), (0,)), ((), ())),
-        preferred_element_type=jnp.float32,
+    sig = jax.nn.sigmoid(pre)
+    hidden = (pre * sig).astype(jnp.bfloat16)
+    pred = jnp.dot(w_rgb[0], xf, precision=high) + jnp.dot(
+        head.T, hidden.astype(jnp.float32), precision=high
     )
-    mixed = xf + delta
-    pred = jnp.dot(w_rgb[0], mixed, precision=lax.Precision.HIGHEST)
     partner = from_partner(pred, "pair", 0)
     pixels_all = pixels * lax.axis_size("dp") * lax.axis_size("fsdp")
     loss_scale = math.sqrt(xf.shape[0] / pixels_all)
     samples = counts.astype(jnp.float32)
     weight = samples / (samples + 64.0)
     g_pred = (weight * (pred - target) + DISTILL * (pred - partner)) * loss_scale
-    g_mixed = jnp.dot(w_rgb[0].T, g_pred, precision=lax.Precision.HIGHEST).astype(jnp.bfloat16)
-    g_hidden = jnp.dot(
-        lax.all_gather(w_down[0], "fsdp", axis=0, tiled=True),
-        g_mixed,
-        preferred_element_type=jnp.float32,
-    )
-    sig = jax.nn.sigmoid(pre)
+    g_hidden = jnp.dot(head, g_pred, precision=high)
     g_pre = (g_hidden * sig * (1.0 + pre * (1.0 - sig))).astype(jnp.bfloat16)
     channels = normed.shape[0]
+    grad_head = lax.dot_general(
+        hidden.astype(jnp.float32), g_pred, (((1,), (1,)), ((), ())), precision=high
+    )
     partial_rows = lax.psum_scatter(
-        jnp.concatenate([contract_rows(g_pre, normed), contract_rows(hidden, g_mixed)], axis=1),
+        jnp.concatenate([contract_rows(g_pre, normed), grad_head], axis=1),
         "fsdp",
         scatter_dimension=0,
         tiled=True,
     )
     totals = lax.psum(partial_rows, "dp")
-    return (pred[None], totals[:, :channels][None], totals[:, channels:][None])
+    grad_down = jnp.dot(totals[:, channels:], w_rgb[0], precision=high)
+    return (pred[None], totals[:, :channels][None], grad_down[None])
 
 
 def solution(mesh):

time: 506 us -> 455 us (0.90)
  the two profiles are of different devices: /device:TPU:1 before, /device:TPU:2 now
where the time goes in v1:
time: 455 us
  waiting for transfers between devices  279 us (61%)
  blocking collectives  133 us (29%)
  matrix products  16.1 us (4%)
  between operations  14.2 us (3%)
  local copies, waits for them, and re-layouts  6.68 us (1%)
    psum x1, waiting for transfers between devices, on_device(): totals = lax.psum(partial_rows, 'dp')  156 us
    unnamed x3, waiting for transfers between devices  122 us
    all_gather x1, blocking collectives, on_device(): lax.all_gather(w_in[0], 'fsdp', axis=0, tiled=True)  74.1 us
    all_gather x1, blocking collectives, on_device(): head = lax.all_gather(head_rows, 'fsdp', axis=0, tiled=True)  58.8 us
  transfers between devices with their start and end apart: 3, of which 3 were waited for; matrix products, arithmetic and copies ran while one was open for 0% of the time, Pallas kernels for 0%

profile of v1, /device:TPU:2, one launch (start us, length us, event | category | flops | bytes accessed | tf_op | source)
XLA Modules:
  0.0 454.9 jit_solution(8733867722866475132)
XLA Ops:
  7.2 0.0 copy-start
  7.2 0.0 reduce-scatter.4.cloned.1.call-start
  7.2 0.8 copy-done
  8.0 0.8 convolution_bitcast_fusion.1
  8.8 58.8 %all-gather.1 = f32[16,80,3]{1,2,0:T(4,128)S(1)} all-gather(f32[1,80,3]{1,2,0:T(4,128)S(1)} %convolution_bitcast_fusion.1), channel_id=1, replica_groups=mesh['pair'=2,'dp'=16,'fsdp'=16] {'fsdp'}, dimensions={0}, use_global_device_ids=true | all-gather | bytes 16320 | tf_op jit(solution)/shard_map/all_gather | solution.py:40
  67.6 0.1 reshape.23
  67.7 74.1 %all-gather = bf16[1,1280,320]{2,1,0:T(8,128)(2,1)S(1)} all-gather(bf16[1,80,320]{2,1,0:T(8,128)(2,1)} %param.11), channel_id=2, replica_groups=mesh['pair'=2,'dp'=16,'fsdp'=16] {'fsdp'}, dimensions={1}, use_global_device_ids=true | all-gather | bytes 870400 | tf_op jit(solution)/shard_map/all_gather | solution.py:42
  141.8 1.3 fusion.24
  143.1 0.6 iota_compare_fusion
  143.8 1.2 fusion.7
  145.0 1.0 select_reduce_fusion
  146.0 3.2 fusion.3
  149.2 0.0 copy-start.1
  149.3 0.0 copy-start.2
  149.3 0.0 copy-start.4
  149.3 0.0 copy-start.3
  149.3 2.1 fusion.25
  151.4 0.0 copy-done.1
  151.4 0.0 copy-done.2
  151.4 0.4 convolution_add_fusion
  151.8 1.9 collective-permute-start
  153.7 0.0 copy-done.4
  153.8 1.1 collective-permute-done
  154.9 0.0 copy-done.3
  154.9 1.1 fusion.26
  156.0 5.7 %fusion.6 = bf16[1280,1024]{0,1:T(8,128)(2,1)S(1)} fusion(f32[1024,1280]{1,0:T(8,128)S(1)} %get-tuple-element.13, f32[1280,3]{0,1:T(4,128)S(1)} %reshape.23, f32[3,1024]{1,0:T(4,128)S(1)} %add_multiply_fusion), kind=kOutput, calls=%fused_computation.9 | convolution fusion | flops 58982400 | bytes 7891968 | tf_op jit(solution)/shard_map/dot_general | solution.py:57
  161.8 1.1 fusion.13
  162.8 0.1 pad_maximum_fusion
  163.0 1.8 copy.21
  164.8 0.0 reduce-scatter.4.cloned.1.call-update
  164.8 0.0 all-reduce.2.cloned.1.call-start
  164.8 121.5 %reduce-scatter.4.cloned.1.call-done = f32[80,323]{1,0:T(8,128)} async-done(((f32[1280,323]{1,0:T(8,128)}), f32[80,323]{1,0:T(8,128)}) %reduce-scatter.4.cloned.1.call-update) | async-done | bytes 103376
  286.3 1.7 copy.22
  288.0 0.0 all-reduce.2.cloned.1.call-update
  288.0 0.6 copy.18
  288.6 156.1 %all-reduce.2.cloned.1.call-done = f32[80,323]{0,1:T(8,128)} async-done(((f32[80,323]{0,1:T(8,128)}), f32[80,323]{0,1:T(8,128)}) %all-reduce.2.cloned.1.call-update) | async-done | bytes 103376 | tf_op jit(solution)/shard_map/psum | solution.py:69
  444.7 0.9 slice_bitcast_fusion
  445.6 0.8 copy.19
  446.4 1.7 convolution_bitcast_fusion
  (4 shorter events, 0.0 us)
Async XLA Ops:
  7.2 0.8 copy-start
  7.2 279.1 %reduce-scatter.4.cloned.1.call-start = ((), (), s32[]{:S(2)}) async-start(), calls=%async_computation.2 | async-start | bytes 2088960
  149.2 2.2 copy-start.1
  149.3 2.2 copy-start.2
  149.3 4.5 copy-start.4
  149.3 5.6 %copy-start.3 = (f32[3,1024]{1,0:T(4,128)S(1)}, f32[3,1024]{1,0:T(4,128)}, u32[]{:S(2)}) copy-start(f32[3,1024]{1,0:T(4,128)} %param.14) | copy-start | bytes 36868
  151.8 3.1 collective-permute-start
  164.8 279.9 %all-reduce.2.cloned.1.call-start = ((), (), s32[]{:S(2)}) async-start(), calls=%async_computation.1 | async-start | bytes 335872 | tf_op jit(solution)/shard_map/psum | solution.py:69
Sparse Core Ops, SparseCore 0:
  164.9 121.3 reduce-scatter.3
  289.5 155.1 all-reduce.1

commit v2 on v1

v2 whole, which is shorter than its diff:
```python
import math

import jax
import jax.numpy as jnp
from jax import lax
from jax.experimental import pallas as pl
from jax.experimental.pallas import tpu as pltpu
from jax.sharding import PartitionSpec as P

IMG_PIX = 4096
EPS = 1e-06
DISTILL = 1.0

MESH = pl.DeviceIdType.MESH
HIGH = lax.Precision.HIGHEST
BF16 = jnp.bfloat16
F32 = jnp.float32

SIDE = 4
OTHERS = SIDE * SIDE - 1
TILE = (16, 128)
BANDS = 5
SLABS = 3
HEAD = 64


def dot(left, right, dims, **kw):
    return lax.dot_general(left, right, (dims, ((), ())), preferred_element_type=F32, **kw)


def kernel(
    loss_scale,
    x_ref, table_ref, levels_ref, w_in_ref, w_down_ref, w_rgb_ref, target_ref, counts_ref,
    pred_ref, grad_in_ref, grad_down_ref,
    rgb, normed, wbuf, wmat, hidden, slope, pred_mine, pred_other, g_rows, g_aug,
    gsend, grecv, zsend, zrecv, fbuf,
    a_send, a_recv, y_send, y_recv, b_send, b_recv, p_send, p_recv,
    r_send, r_recv, z_send, z_recv, f_send, f_recv,
):
    pair = lax.axis_index("pair")
    dp = lax.axis_index("dp")
    fsdp = lax.axis_index("fsdp")
    x, zl = dp // SIDE, dp % SIDE
    y, zh = fsdp // SIDE, fsdp % SIDE
    here = y * SIDE + x
    pixels = x_ref.shape[1]
    channels = x_ref.shape[0]
    rows = w_in_ref.shape[0]

    def device(x_, y_, zh_, zl_):
        return (pair, x_ * SIDE + zl_, y_ * SIDE + zh_)

    def plane_peer(i):
        return device((x + i % SIDE) % SIDE, (y + i // SIDE) % SIDE, zh, zl)

    def z_peer(i):
        return device(x, y, (zh + i // SIDE) % SIDE, (zl + i % SIDE) % SIDE)

    def dp_peer(i):
        return device((x + i // SIDE) % SIDE, y, zh, (zl + i % SIDE) % SIDE)

    barrier = pltpu.get_barrier_semaphore()

    def greet(peer):
        pl.semaphore_signal(barrier, inc=1, device_id=peer, device_id_type=MESH)

    def greet_all(i, carry):
        greet(plane_peer(i))
        greet(z_peer(i))
        return carry

    lax.fori_loop(1, OTHERS + 1, greet_all, 0)
    for a in range(1, SIDE):
        for b in range(1, SIDE):
            greet(dp_peer(a * SIDE + b))
    greet((1 - pair, dp, fsdp))

    rgb[...] = jnp.zeros_like(rgb)
    for copy in range(3):
        rgb[HEAD + 3 * copy : HEAD + 3 * copy + 3, :] = w_rgb_ref[...]
    lane = lax.broadcasted_iota(jnp.int32, (rows, 128), 1)
    head = dot(w_down_ref[...].astype(F32), rgb[...], ((1,), (1,)), precision=HIGH)
    head_hi = head.astype(BF16).astype(F32)
    is_lo = (lane >= HEAD + 3) & (lane < HEAD + 6)
    head = jnp.where(is_lo, head - head_hi, head_hi)
    w_own = w_in_ref[...]
    last = w_own[:, 256:320].astype(F32)
    last = jnp.concatenate([last, jnp.zeros((rows, 64), F32)], axis=1) + head
    slabs = [w_own[:, 0:128], w_own[:, 128:256], last.astype(BF16)]
    own_quarters = wbuf.at[zh]
    for band in range(BANDS):
        for slab in range(SLABS):
            q = band * SLABS + slab
            own_quarters[y * SIDE + q // SIDE, q % SIDE] = slabs[slab][16 * band : 16 * band + 16, :]
    own_quarters[y * SIDE + SIDE - 1, SIDE - 1] = jnp.zeros(TILE, BF16)

    pl.semaphore_wait(barrier, 2 * OTHERS + 9 + 1)

    def remote(src, dst, send, recv, peer):
        return pltpu.make_async_remote_copy(
            src_ref=src, dst_ref=dst, send_sem=send, recv_sem=recv,
            device_id=peer, device_id_type=MESH,
        )

    def wait_bytes(ref, sem):
        pltpu.make_async_copy(ref, ref, sem).wait()

    far_first = (2, 1, 3)
    quarter = wbuf.at[zh, here]
    along_z = {}
    for k in far_first:
        along_z[k] = remote(quarter, quarter, a_send.at[k], a_recv.at[k], device(x, y, (zh + k) % SIDE, zl))
        along_z[k].start()
    block = wbuf.at[zh, pl.ds(y * SIDE, SIDE)]
    along_y = []
    for m in range(1, SIDE):
        c = remote(block, block, y_send.at[m], y_recv.at[m], device(x, (y + m) % SIDE, zh, zl))
        c.start()
        along_y.append(c)

    image = ((dp * SIDE * SIDE + fsdp) * pixels) // IMG_PIX
    levels = levels_ref[...].astype(F32)
    spots = lax.broadcasted_iota(jnp.int32, levels.shape, 1)
    level = jnp.sum(jnp.where(spots == image, levels, 0.0), axis=1, keepdims=True)
    table_rows = lax.broadcasted_iota(jnp.int32, table_ref.shape, 0).astype(F32)
    gain = jnp.sum(jnp.where(table_rows == level, table_ref[...], 0.0), axis=0, keepdims=True)
    gain = jnp.concatenate([gain, jnp.zeros((1, 384 - channels), F32)], axis=1)
    gain = jnp.broadcast_to(gain, (128, 384)).T[:channels, 0:1]
    xf = x_ref[...].astype(F32)
    mean_sq = jnp.mean(xf * xf, axis=0, keepdims=True)
    normed[0:channels, :] = (xf * lax.rsqrt(mean_sq + EPS) * gain).astype(BF16)
    normed[channels:, :] = jnp.zeros((384 - channels, pixels), BF16)

    part = rgb[HEAD : HEAD + 16, :]
    part_hi = part.astype(BF16).astype(F32)
    part_mid = (part - part_hi).astype(BF16).astype(F32)
    part_lo = part - part_hi - part_mid
    row = lax.broadcasted_iota(jnp.int32, part.shape, 0)
    part = jnp.where(row < 3, part_hi, jnp.where(row < 6, part_mid, part_lo)).astype(BF16)
    direct = dot(part, x_ref[...], ((1,), (0,)))
    pred_mine[...] = jnp.zeros_like(pred_mine)
    pred_mine[0:3, :] = direct[0:3] + direct[3:6] + direct[6:9]

    wide = 256

    def forward(group):
        def assemble(yy, carry):
            for band in range(BANDS):
                for slab in range(SLABS):
                    q = band * SLABS + slab
                    wmat[group, pl.ds(yy * rows + 16 * band, 16), 128 * slab : 128 * slab + 128] = (
                        wbuf[group, yy * SIDE + q // SIDE, q % SIDE]
                    )
            return carry

        lax.fori_loop(0, SIDE, assemble, 0)

        def columns(n, carry):
            at = pl.ds(pl.multiple_of(n * wide, wide), wide)
            pre = dot(wmat[group], normed[:, at], ((1,), (0,)))
            sig = jax.nn.sigmoid(pre)
            hid = (pre * sig).astype(BF16)
            hidden[group, :, at] = hid
            slope[group, :, at] = sig * (1.0 + pre * (1.0 - sig))
            through = dot(wmat[group, :, 256:384], hid, ((0,), (0,)))
            pred_mine[0:3, at] += through[HEAD : HEAD + 3] + through[HEAD + 3 : HEAD + 6]
            return carry

        lax.fori_loop(0, pixels // wide, columns, 0)

    def forward_on(k):
        group = (zh + SIDE - k) % SIDE
        along_z[k].wait_recv()
        chunk = wbuf.at[group, here]

        def send(i, carry):
            remote(chunk, chunk, b_send.at[k], b_recv.at[k], plane_peer(i)).start()
            return carry

        lax.fori_loop(1, OTHERS + 1, send, 0)

    for c in along_y:
        c.wait_recv()
    for k in (1, 3, 2):
        forward_on(k)
    forward(zh)
    for k in (1, 3, 2):
        wait_bytes(wbuf.at[0, 0:OTHERS], b_recv.at[k])
        forward((zh + SIDE - k) % SIDE)

    swap = remote(pred_mine, pred_other, p_send, p_recv, (1 - pair, dp, fsdp))
    swap.start()
    pred = pred_mine[0:3, :]
    pred_ref[...] = pred
    samples = counts_ref[...].astype(F32)
    weight = samples / (samples + 64.0)
    toward = weight * (pred - target_ref[...])
    swap.wait_recv()
    g_pred = (toward + DISTILL * (pred - pred_other[0:3, :])) * loss_scale
    g_hi = g_pred.astype(BF16).astype(F32)
    g_rows[...] = jnp.zeros_like(g_rows)
    g_rows[0:3, :] = g_hi
    g_rows[3:6, :] = g_hi
    g_rows[6:9, :] = g_pred - g_hi
    g_aug[...] = jnp.zeros_like(g_aug)
    g_aug[HEAD : HEAD + 16, :] = g_rows[...].astype(BF16)

    lane_g = lax.broadcasted_iota(jnp.int32, (SIDE * rows, 128), 1)
    is_rest = (lane_g >= HEAD + 3) & (lane_g < HEAD + 6)

    def backward(group):
        g_hidden = dot(wmat[group, :, 256:384], g_aug[...], ((1,), (0,)))
        g_pre = (g_hidden * slope[group]).astype(BF16)
        grad = dot(g_pre, normed[...], ((1,), (1,)))
        for_head = dot(hidden[group], g_aug[...], ((1,), (1,)))
        for_head = jnp.where(is_rest, for_head - for_head.astype(BF16).astype(F32), for_head)
        out = [
            grad[:, 0:128].astype(BF16),
            grad[:, 128:256].astype(BF16),
            (grad[:, 256:384] + for_head).astype(BF16),
        ]
        for yy in range(SIDE):
            for band in range(BANDS):
                for slab in range(SLABS):
                    q = band * SLABS + slab
                    top = yy * rows + 16 * band
                    gsend[group, yy * SIDE + q // SIDE, q % SIDE] = out[slab][top : top + 16, :]
            gsend[group, yy * SIDE + SIDE - 1, SIDE - 1] = jnp.zeros(TILE, BF16)

        def send(i, carry):
            there = ((y + i // SIDE) % SIDE) * SIDE + (x + i % SIDE) % SIDE
            remote(
                gsend.at[group, there], grecv.at[group, here],
                r_send.at[group], r_recv.at[group], plane_peer(i),
            ).start()
            return carry

        lax.fori_loop(1, OTHERS + 1, send, 0)
        grecv[group, here] = gsend[group, here]

    order = [(zh + k) % SIDE for k in (2, 1, 3, 0)]

    def plane_sum(k, group):
        wait_bytes(grecv.at[0, 0:OTHERS], r_recv.at[group])
        total = grecv[group, 0].astype(F32)
        for s in range(1, SIDE * SIDE):
            total = total + grecv[group, s].astype(F32)
        zsend[group] = total

        def send(b, carry):
            to = (zl + b) % SIDE
            remote(
                zsend.at[group, to], zrecv.at[zh * SIDE + zl], z_send, z_recv, device(x, y, group, to)
            ).start()
            return carry

        lax.fori_loop(1 if k == 0 else 0, SIDE, send, 0)

    for group in order:
        backward(group)
    for k, group in zip((2, 1, 3, 0), order):
        plane_sum(k, group)
    zrecv[zh * SIDE + zl] = zsend[zh, zl]
    wait_bytes(zrecv.at[0:OTHERS], z_recv)
    total = zrecv[0]
    for s in range(1, SIDE * SIDE):
        total = total + zrecv[s]
    own = dp
    fbuf[own] = total

    def send_piece(i, carry):
        remote(fbuf.at[own], fbuf.at[own], f_send, f_recv, dp_peer(i)).start()
        return carry

    lax.fori_loop(1, OTHERS + 1, send_piece, 0)

    for k in far_first:
        along_z[k].wait_send()
        wait_bytes(wbuf.at[0, 0:OTHERS], b_send.at[k])
    for c in along_y:
        c.wait_send()
    swap.wait_send()
    for group in range(SIDE):
        wait_bytes(gsend.at[0, 0:OTHERS], r_send.at[group])
    wait_bytes(zrecv.at[0:OTHERS], z_send)

    wait_bytes(fbuf.at[0:OTHERS], f_recv)
    for band in range(BANDS):
        at = slice(16 * band, 16 * band + 16)
        grad_in_ref[at, 0:128] = fbuf[band * SLABS]
        grad_in_ref[at, 128:256] = fbuf[band * SLABS + 1]
        grad_in_ref[at, 256:320] = fbuf[band * SLABS + 2][:, 0:64]
        grad_down_ref[at, :] = dot(fbuf[band * SLABS + 2], rgb[...], ((1,), (0,)), precision=HIGH)
    wait_bytes(fbuf.at[0:OTHERS], f_send)


def on_device(loss_scale, features, level_gain, levels, w_in, w_down, w_rgb, target, counts):
    channels, pixels = features.shape[1:]
    rows = w_in.shape[1]
    all_rows = SIDE * SIDE * rows
    group_rows = SIDE * rows
    plane = SIDE * SIDE
    dma = pltpu.SemaphoreType.DMA
    vmem = pl.BlockSpec(memory_space=pltpu.VMEM)
    flops = 2 * all_rows * pixels * (2 * 384 + 3 * 128)
    pred, grad_in, grad_down = pl.pallas_call(
        lambda *refs: kernel(loss_scale, *refs),
        out_shape=(
            jax.ShapeDtypeStruct((3, pixels), F32),
            jax.ShapeDtypeStruct((rows, channels), F32),
            jax.ShapeDtypeStruct((rows, channels), F32),
        ),
        in_specs=[vmem] * 8,
        out_specs=(vmem, vmem, vmem),
        scratch_shapes=[
            pltpu.VMEM((128, channels), F32),
            pltpu.VMEM((384, pixels), BF16),
            pltpu.VMEM((SIDE, plane, SIDE, *TILE), BF16),
            pltpu.VMEM((SIDE, group_rows, 384), BF16),
            pltpu.VMEM((SIDE, group_rows, pixels), BF16),
            pltpu.VMEM((SIDE, group_rows, pixels), F32),
            pltpu.VMEM((8, pixels), F32),
            pltpu.VMEM((8, pixels), F32),
            pltpu.VMEM((16, pixels), F32),
            pltpu.VMEM((128, pixels), BF16),
            pltpu.VMEM((SIDE, plane, SIDE, *TILE), BF16),
            pltpu.VMEM((SIDE, plane, SIDE, *TILE), BF16),
            pltpu.VMEM((SIDE, SIDE, *TILE), F32),
            pltpu.VMEM((plane, *TILE), F32),
            pltpu.VMEM((plane, *TILE), F32),
            dma((SIDE,)), dma((SIDE,)), dma((SIDE,)), dma((SIDE,)), dma((SIDE,)), dma((SIDE,)), dma, dma,
            dma((SIDE,)), dma((SIDE,)), dma, dma, dma, dma,
        ],
        compiler_params=pltpu.CompilerParams(
            collective_id=0, has_side_effects=True, vmem_limit_bytes=56 * 2**20
        ),
        cost_estimate=pl.CostEstimate(flops=flops, bytes_accessed=2**21, transcendentals=all_rows * pixels),
    )(features[0], level_gain, levels[None], w_in[0], w_down[0], w_rgb[0], target, counts[None])
    return pred[None], grad_in[None], grad_down[None]


def solution(mesh):
    in_specs = (
        P("pair", None, ("dp", "fsdp")),
        P(),
        P(),
        P("pair", "fsdp", None),
        P("pair", "fsdp", None),
        P("pair", None, None),
        P(None, ("dp", "fsdp")),
        P(("dp", "fsdp")),
    )
    out_specs = (P("pair", None, ("dp", "fsdp")), P("pair", "fsdp", None), P("pair", "fsdp", None))

    def whole(features, *rest):
        loss_scale = math.sqrt(features.shape[1] / features.shape[2])
        return jax.shard_map(
            lambda *args: on_device(loss_scale, *args),
            mesh=mesh, in_specs=in_specs, out_specs=out_specs, check_vma=False,
        )(features, *rest)

    return whole
```

time: 455 us -> 71.6 us (0.16)
  the two profiles are of different devices: /device:TPU:2 before, /device:TPU:1 now
where the time goes in v2:
time: 71.6 us; the launch traced here: 71.3 us
  Pallas kernels  65.8 us (92%)
  local copies, waits for them, and re-layouts  4.85 us (7%)
    pallas_call x1, Pallas kernels, on_device(): pl.pallas_call(lambda *refs: kernel(loss_scale, *refs), out_shape=(jax.Sh...  65.8 us
    unnamed x8, local copies, waits for them, and re-layouts  4.85 us

profile of v2, /device:TPU:1, one launch (start us, length us, event | category | flops | bytes accessed | tf_op | source)
XLA Modules:
  0.0 71.3 jit_solution(10180671140778595089)
XLA Ops:
  0.6 0.0 copy-start.1
  0.6 0.7 copy-done.1
  1.3 0.6 copy.14
  1.9 65.8 %shard_map.103 = (f32[3,1024]{1,0:T(4,128)}, f32[80,320]{1,0:T(8,128)}, f32[80,320]{1,0:T(8,128)}) custom-call(bf16[320,1024]{1,0:T(8,128)(2,1)} %bitcast.15, f32[64,320]{1,0:T(8,128)} %refs_1_.1, s32[1,64]{1,0:T(1,128)} %bitcast.19, bf16[80,320]{1,0:T(8,128)(2,1)} %bitcast.16, bf16[80,320]{1,0:T(8,128)(2,1)} %bitcast.17, f32[3,320]{1,0:T(4,128)} %bitcast.14, ...), custom_call_target="tpu_custom_call" | custom-call | flops 3019898880 | bytes 2097152 | tf_op jit(solution)/shard_map/pallas_call | solution.py:306
  67.8 1.3 %copy.11 = f32[1,3,1024]{2,0,1:T(1,128)} copy(f32[1,3,1024]{2,1,0:T(4,128)} %bitcast.13) | data formatting | bytes 24576
  69.1 0.0 copy-start
  69.1 1.6 %copy.17 = f32[1,80,320]{2,1,0:T(8,128)} copy(f32[1,80,320]{2,1,0:T(8,128)} %bitcast.12) | data formatting | bytes 204800
  70.7 0.0 copy-done
  70.7 0.6 copy.18
Async XLA Ops:
  0.6 0.7 copy-start.1
  69.1 1.6 %copy-start = (f32[80,320]{1,0:T(8,128)S(1)}, f32[80,320]{1,0:T(8,128)}, u32[]{:S(2)}) copy-start(f32[80,320]{1,0:T(8,128)} %get-tuple-element.8) | copy-start | bytes 307204

commit v3 on v2

--- a/solution.py
+++ b/solution.py
@@ -31,10 +31,10 @@
 def kernel(
     loss_scale,
     x_ref, table_ref, levels_ref, w_in_ref, w_down_ref, w_rgb_ref, target_ref, counts_ref,
-    pred_ref, grad_in_ref, grad_down_ref,
-    rgb, normed, wbuf, wmat, hidden, slope, pred_mine, pred_other, g_rows, g_aug,
+    pred_ref, sums_ref,
+    rgb, normed, wbuf, wmat, head_t, hidden, slope, pred_mine, pred_other, g_rows, g_aug,
     gsend, grecv, zsend, zrecv, fbuf,
-    a_send, a_recv, y_send, y_recv, b_send, b_recv, p_send, p_recv,
+    a_send, a_recv, e_send, e_recv, y_send, y_recv, b_send, b_recv, p_send, p_recv,
     r_send, r_recv, z_send, z_recv, f_send, f_recv,
 ):
     pair = lax.axis_index("pair")
@@ -59,6 +59,9 @@
     def dp_peer(i):
         return device((x + i // SIDE) % SIDE, y, zh, (zl + i % SIDE) % SIDE)
 
+    def group_peer(k):
+        return device(x, y, (zh + k) % SIDE, zl)
+
     barrier = pltpu.get_barrier_semaphore()
 
     def greet(peer):
@@ -66,18 +69,21 @@
 
     def greet_all(i, carry):
         greet(plane_peer(i))
-        greet(z_peer(i))
         return carry
 
     lax.fori_loop(1, OTHERS + 1, greet_all, 0)
-    for a in range(1, SIDE):
+    for a in range(SIDE):
         for b in range(1, SIDE):
             greet(dp_peer(a * SIDE + b))
+    for k in (1, 3):
+        greet(group_peer(k))
     greet((1 - pair, dp, fsdp))
 
     rgb[...] = jnp.zeros_like(rgb)
     for copy in range(3):
-        rgb[HEAD + 3 * copy : HEAD + 3 * copy + 3, :] = w_rgb_ref[...]
+        for k in range(3):
+            at = HEAD + 3 * copy + k
+            rgb[at : at + 1, :] = w_rgb_ref[k]
     lane = lax.broadcasted_iota(jnp.int32, (rows, 128), 1)
     head = dot(w_down_ref[...].astype(F32), rgb[...], ((1,), (1,)), precision=HIGH)
     head_hi = head.astype(BF16).astype(F32)
@@ -94,7 +100,7 @@
             own_quarters[y * SIDE + q // SIDE, q % SIDE] = slabs[slab][16 * band : 16 * band + 16, :]
     own_quarters[y * SIDE + SIDE - 1, SIDE - 1] = jnp.zeros(TILE, BF16)
 
-    pl.semaphore_wait(barrier, 2 * OTHERS + 9 + 1)
+    pl.semaphore_wait(barrier, OTHERS + 12 + 2 + 1)
 
     def remote(src, dst, send, recv, peer):
         return pltpu.make_async_remote_copy(
@@ -105,11 +111,10 @@
     def wait_bytes(ref, sem):
         pltpu.make_async_copy(ref, ref, sem).wait()
 
-    far_first = (2, 1, 3)
     quarter = wbuf.at[zh, here]
     along_z = {}
-    for k in far_first:
-        along_z[k] = remote(quarter, quarter, a_send.at[k], a_recv.at[k], device(x, y, (zh + k) % SIDE, zl))
+    for k in (1, 3):
+        along_z[k] = remote(quarter, quarter, a_send.at[k], a_recv.at[k], group_peer(k))
         along_z[k].start()
     block = wbuf.at[zh, pl.ds(y * SIDE, SIDE)]
     along_y = []
@@ -154,23 +159,32 @@
             return carry
 
         lax.fori_loop(0, SIDE, assemble, 0)
+        head_t[group] = wmat[group, :, 256:384].astype(F32).T[HEAD : HEAD + 16].astype(BF16)
 
         def columns(n, carry):
             at = pl.ds(pl.multiple_of(n * wide, wide), wide)
             pre = dot(wmat[group], normed[:, at], ((1,), (0,)))
-            sig = jax.nn.sigmoid(pre)
-            hid = (pre * sig).astype(BF16)
+            sig = 0.5 * jnp.tanh(0.5 * pre) + 0.5
+            act = pre * sig
+            hid = act.astype(BF16)
             hidden[group, :, at] = hid
-            slope[group, :, at] = sig * (1.0 + pre * (1.0 - sig))
-            through = dot(wmat[group, :, 256:384], hid, ((0,), (0,)))
-            pred_mine[0:3, at] += through[HEAD : HEAD + 3] + through[HEAD + 3 : HEAD + 6]
+            slope[group, :, at] = sig + act * (1.0 - sig)
+            through = dot(head_t[group], hid, ((1,), (0,)))
+            pred_mine[0:3, at] += through[0:3] + through[3:6]
             return carry
 
-        lax.fori_loop(0, pixels // wide, columns, 0)
+        lax.fori_loop(0, pixels // wide, columns, 0, unroll=True)
 
     def forward_on(k):
         group = (zh + SIDE - k) % SIDE
-        along_z[k].wait_recv()
+        if k == 2:
+            relays[1].wait_recv()
+            relays[3].wait_recv()
+        else:
+            along_z[k].wait_recv()
+            half = wbuf.at[group, here, pl.ds(0 if k == 1 else 2, 2)]
+            relays[k] = remote(half, half, e_send.at[k], e_recv.at[k], group_peer(k))
+            relays[k].start()
         chunk = wbuf.at[group, here]
 
         def send(i, carry):
@@ -179,11 +193,13 @@
 
         lax.fori_loop(1, OTHERS + 1, send, 0)
 
+    relays = {}
+    for k in (1, 3):
+        forward_on(k)
     for c in along_y:
         c.wait_recv()
-    for k in (1, 3, 2):
-        forward_on(k)
     forward(zh)
+    forward_on(2)
     for k in (1, 3, 2):
         wait_bytes(wbuf.at[0, 0:OTHERS], b_recv.at[k])
         forward((zh + SIDE - k) % SIDE)
@@ -191,7 +207,8 @@
     swap = remote(pred_mine, pred_other, p_send, p_recv, (1 - pair, dp, fsdp))
     swap.start()
     pred = pred_mine[0:3, :]
-    pred_ref[...] = pred
+    for k in range(3):
+        pred_ref[k] = pred[k : k + 1]
     samples = counts_ref[...].astype(F32)
     weight = samples / (samples + 64.0)
     toward = weight * (pred - target_ref[...])
@@ -274,8 +291,10 @@
 
     lax.fori_loop(1, OTHERS + 1, send_piece, 0)
 
-    for k in far_first:
-        along_z[k].wait_send()
+    for k in (1, 2, 3):
+        if k != 2:
+            along_z[k].wait_send()
+            relays[k].wait_send()
         wait_bytes(wbuf.at[0, 0:OTHERS], b_send.at[k])
     for c in along_y:
         c.wait_send()
@@ -285,13 +304,24 @@
     wait_bytes(zrecv.at[0:OTHERS], z_send)
 
     wait_bytes(fbuf.at[0:OTHERS], f_recv)
+    sums_ref[...] = fbuf[...]
+    wait_bytes(fbuf.at[0:OTHERS], f_send)
+
+
+def results(sums_ref, pred_in_ref, w_rgb_ref, pred_ref, grad_in_ref, grad_down_ref, rgb):
+    pred_ref[...] = pred_in_ref[...]
+    rgb[...] = jnp.zeros_like(rgb)
+    for copy in range(3):
+        for k in range(3):
+            at = HEAD + 3 * copy + k
+            rgb[at : at + 1, :] = w_rgb_ref[k]
     for band in range(BANDS):
         at = slice(16 * band, 16 * band + 16)
-        grad_in_ref[at, 0:128] = fbuf[band * SLABS]
-        grad_in_ref[at, 128:256] = fbuf[band * SLABS + 1]
-        grad_in_ref[at, 256:320] = fbuf[band * SLABS + 2][:, 0:64]
-        grad_down_ref[at, :] = dot(fbuf[band * SLABS + 2], rgb[...], ((1,), (0,)), precision=HIGH)
-    wait_bytes(fbuf.at[0:OTHERS], f_send)
+        grad_in_ref[at, 0:128] = sums_ref[band * SLABS]
+        grad_in_ref[at, 128:256] = sums_ref[band * SLABS + 1]
+        grad_in_ref[at, 256:320] = sums_ref[band * SLABS + 2][:, 0:64]
+    last = jnp.concatenate([sums_ref[band * SLABS + 2] for band in range(BANDS)], axis=0)
+    grad_down_ref[...] = dot(last, rgb[...], ((1,), (0,)), precision=HIGH)
 
 
 def on_device(loss_scale, features, level_gain, levels, w_in, w_down, w_rgb, target, counts):
@@ -303,20 +333,21 @@
     dma = pltpu.SemaphoreType.DMA
     vmem = pl.BlockSpec(memory_space=pltpu.VMEM)
     flops = 2 * all_rows * pixels * (2 * 384 + 3 * 128)
-    pred, grad_in, grad_down = pl.pallas_call(
+    colours = jnp.transpose(w_rgb, (1, 0, 2))
+    pred, sums = pl.pallas_call(
         lambda *refs: kernel(loss_scale, *refs),
         out_shape=(
-            jax.ShapeDtypeStruct((3, pixels), F32),
-            jax.ShapeDtypeStruct((rows, channels), F32),
-            jax.ShapeDtypeStruct((rows, channels), F32),
+            jax.ShapeDtypeStruct((3, 1, pixels), F32),
+            jax.ShapeDtypeStruct((plane, *TILE), F32),
         ),
         in_specs=[vmem] * 8,
-        out_specs=(vmem, vmem, vmem),
+        out_specs=(vmem, vmem),
         scratch_shapes=[
             pltpu.VMEM((128, channels), F32),
             pltpu.VMEM((384, pixels), BF16),
             pltpu.VMEM((SIDE, plane, SIDE, *TILE), BF16),
             pltpu.VMEM((SIDE, group_rows, 384), BF16),
+            pltpu.VMEM((SIDE, 16, group_rows), BF16),
             pltpu.VMEM((SIDE, group_rows, pixels), BF16),
             pltpu.VMEM((SIDE, group_rows, pixels), F32),
             pltpu.VMEM((8, pixels), F32),
@@ -328,15 +359,27 @@
             pltpu.VMEM((SIDE, SIDE, *TILE), F32),
             pltpu.VMEM((plane, *TILE), F32),
             pltpu.VMEM((plane, *TILE), F32),
-            dma((SIDE,)), dma((SIDE,)), dma((SIDE,)), dma((SIDE,)), dma((SIDE,)), dma((SIDE,)), dma, dma,
+            dma((SIDE,)), dma((SIDE,)), dma((SIDE,)), dma((SIDE,)),
+            dma((SIDE,)), dma((SIDE,)), dma((SIDE,)), dma((SIDE,)), dma, dma,
             dma((SIDE,)), dma((SIDE,)), dma, dma, dma, dma,
         ],
         compiler_params=pltpu.CompilerParams(
             collective_id=0, has_side_effects=True, vmem_limit_bytes=56 * 2**20
         ),
         cost_estimate=pl.CostEstimate(flops=flops, bytes_accessed=2**21, transcendentals=all_rows * pixels),
-    )(features[0], level_gain, levels[None], w_in[0], w_down[0], w_rgb[0], target, counts[None])
-    return pred[None], grad_in[None], grad_down[None]
+    )(features[0], level_gain, levels[None], w_in[0], w_down[0], colours, target, counts[None])
+    pred, grad_in, grad_down = pl.pallas_call(
+        results,
+        out_shape=(
+            jax.ShapeDtypeStruct((3, 1, pixels), F32),
+            jax.ShapeDtypeStruct((rows, channels), F32),
+            jax.ShapeDtypeStruct((rows, channels), F32),
+        ),
+        in_specs=[vmem] * 3,
+        out_specs=(vmem, vmem, vmem),
+        scratch_shapes=[pltpu.VMEM((128, channels), F32)],
+    )(sums, pred, colours)
+    return jnp.transpose(pred, (1, 0, 2)), grad_in[None], grad_down[None]
 
 
 def solution(mesh):

time: 71.6 us -> 61.8 us (0.86)
  local copies, waits for them, and re-layouts: 4.85 us -> 0 us
  Pallas kernels: 65.8 us -> 61 us
    pallas_call x1, Pallas kernels: 65.8 us -> 59.1 us  [on_device(): pl.pallas_call(lambda *refs: kernel(loss_scale, *refs), out_shape=(jax.Sh...]
    unnamed x8 -> x0, local copies, waits for them, and re-layouts: 4.85 us -> none
    pallas_call x0 -> x1, Pallas kernels: none -> 1.84 us  [on_device(): pl.pallas_call(results, out_shape=(jax.ShapeDtypeStruct((3, 1, pixels), F...]
where the time goes in v3:
time: 61.8 us; the launch traced here: 61.6 us
  Pallas kernels  61 us (99%)
  between operations  0.64 us (1%)
    pallas_call x1, Pallas kernels, on_device(): pl.pallas_call(lambda *refs: kernel(loss_scale, *refs), out_shape=(jax.Sh...  59.1 us
    pallas_call x1, Pallas kernels, on_device(): pl.pallas_call(results, out_shape=(jax.ShapeDtypeStruct((3, 1, pixels), F...  1.84 us

profile of v3, /device:TPU:1, one launch (start us, length us, event | category | flops | bytes accessed | tf_op | source)
XLA Modules:
  0.0 61.6 jit_solution(16344880397330961317)
XLA Ops:
  0.6 59.1 %shard_map.103 = (f32[3,1,1024]{2,1,0:T(1,128)}, f32[16,16,128]{2,1,0:T(8,128)}) custom-call(bf16[320,1024]{1,0:T(8,128)(2,1)} %bitcast.11, f32[64,320]{1,0:T(8,128)} %refs_1_.1, s32[1,64]{1,0:T(1,128)} %bitcast.18, bf16[80,320]{1,0:T(8,128)(2,1)} %bitcast.14, bf16[80,320]{1,0:T(8,128)(2,1)} %bitcast.15, f32[3,1,320]{2,1,0:T(1,128)} %bitcast.9, ...), custom_call_target="tpu_custom_call" | custom-call | flops 3019898880 | bytes 2097152 | tf_op jit(solution)/shard_map/pallas_call | solution.py:337
  59.8 1.8 %shard_map.104 = (f32[3,1,1024]{2,1,0:T(1,128)}, f32[80,320]{1,0:T(8,128)}, f32[80,320]{1,0:T(8,128)}) custom-call(f32[16,16,128]{2,1,0:T(8,128)} %get-tuple-element.8.sums_ref, f32[3,1,1024]{2,1,0:T(1,128)} %get-tuple-element.9.pred_in_ref, f32[3,1,320]{2,1,0:T(1,128)} %bitcast.10), custom_call_target="tpu_custom_call" | custom-call | tf_op jit(solution)/shard_map/pallas_call | solution.py:371

commit v4 on v3

--- a/solution.py
+++ b/solution.py
@@ -20,8 +20,28 @@
 OTHERS = SIDE * SIDE - 1
 TILE = (16, 128)
 BANDS = 5
-SLABS = 3
 HEAD = 64
+PARTS = 9
+SHARE = 3
+TILES = SIDE * SHARE + 1
+
+
+def pack(slab0, slab1, last, head):
+    band = [slice(16 * b, 16 * b + 16) for b in range(BANDS)]
+    tiles = [slab0[at] for at in band] + [slab1[at] for at in band]
+    tiles.append(last[band[0]] + pltpu.roll(last[band[1]], 64, 1))
+    tiles.append(last[band[2]] + pltpu.roll(last[band[3]], 64, 1))
+    end = last[band[4]] + head[band[0]]
+    for b in range(1, BANDS):
+        end = end + pltpu.roll(head[band[b]], PARTS * b, 1)
+    return [t.astype(BF16) for t in tiles] + [end.astype(BF16)]
+
+
+def unpack_last(ten, eleven, end):
+    lane = lax.broadcasted_iota(jnp.int32, TILE, 1)
+    values = [ten, pltpu.roll(ten, 64, 1), eleven, pltpu.roll(eleven, 64, 1), end]
+    heads = [end] + [pltpu.roll(end, 128 - PARTS * b, 1) for b in range(1, BANDS)]
+    return [jnp.where(lane < HEAD, v, h) for v, h in zip(values, heads)]
 
 
 def dot(left, right, dims, **kw):
@@ -32,8 +52,9 @@
     loss_scale,
     x_ref, table_ref, levels_ref, w_in_ref, w_down_ref, w_rgb_ref, target_ref, counts_ref,
     pred_ref, sums_ref,
-    rgb, normed, wbuf, wmat, head_t, hidden, slope, pred_mine, pred_other, g_rows, g_aug,
-    gsend, grecv, zsend, zrecv, fbuf,
+    rgb, normed, wbuf, wext, wmat, head_t, hidden, slope, pred_mine, pred_other, g_rows, g_aug,
+    gsend, gext, grecv, xrecv, zsend, zext, zrecv, fbuf,
+    ax_send, ax_recv, ex_send, ex_recv, yx_send, yx_recv, bx_send, bx_recv, rx_send, rx_recv,
     a_send, a_recv, e_send, e_recv, y_send, y_recv, b_send, b_recv, p_send, p_recv,
     r_send, r_recv, z_send, z_recv, f_send, f_recv,
 ):
@@ -91,14 +112,11 @@
     head = jnp.where(is_lo, head - head_hi, head_hi)
     w_own = w_in_ref[...]
     last = w_own[:, 256:320].astype(F32)
-    last = jnp.concatenate([last, jnp.zeros((rows, 64), F32)], axis=1) + head
-    slabs = [w_own[:, 0:128], w_own[:, 128:256], last.astype(BF16)]
-    own_quarters = wbuf.at[zh]
-    for band in range(BANDS):
-        for slab in range(SLABS):
-            q = band * SLABS + slab
-            own_quarters[y * SIDE + q // SIDE, q % SIDE] = slabs[slab][16 * band : 16 * band + 16, :]
-    own_quarters[y * SIDE + SIDE - 1, SIDE - 1] = jnp.zeros(TILE, BF16)
+    last = jnp.concatenate([last, jnp.zeros((rows, 64), F32)], axis=1)
+    tiles = pack(w_own[:, 0:128], w_own[:, 128:256], last, head)
+    for t in range(TILES - 1):
+        wbuf[zh, y * SIDE + t // SHARE, t % SHARE] = tiles[t]
+    wext[zh, y] = tiles[-1]
 
     pl.semaphore_wait(barrier, OTHERS + 12 + 2 + 1)
 
@@ -116,10 +134,24 @@
     for k in (1, 3):
         along_z[k] = remote(quarter, quarter, a_send.at[k], a_recv.at[k], group_peer(k))
         along_z[k].start()
+
+    def when_mine(group, copy):
+        @pl.when(x == group)
+        def _():
+            copy()
+
+    along_z_ext = {}
+    for k in (1, 3):
+        along_z_ext[k] = remote(wext.at[zh, y], wext.at[zh, y], ax_send.at[k], ax_recv.at[k], group_peer(k))
+        when_mine(zh, along_z_ext[k].start)
     block = wbuf.at[zh, pl.ds(y * SIDE, SIDE)]
     along_y = []
     for m in range(1, SIDE):
         c = remote(block, block, y_send.at[m], y_recv.at[m], device(x, (y + m) % SIDE, zh, zl))
+        c.start()
+        along_y.append(c)
+        peer = device(x, (y + m) % SIDE, zh, zl)
+        c = remote(wext.at[zh, y], wext.at[zh, y], yx_send.at[m], yx_recv.at[m], peer)
         c.start()
         along_y.append(c)
 
@@ -150,12 +182,15 @@
 
     def forward(group):
         def assemble(yy, carry):
+            def tile(t):
+                return wbuf[group, yy * SIDE + t // SHARE, t % SHARE]
+
+            end = unpack_last(tile(10).astype(F32), tile(11).astype(F32), wext[group, yy].astype(F32))
             for band in range(BANDS):
-                for slab in range(SLABS):
-                    q = band * SLABS + slab
-                    wmat[group, pl.ds(yy * rows + 16 * band, 16), 128 * slab : 128 * slab + 128] = (
-                        wbuf[group, yy * SIDE + q // SIDE, q % SIDE]
-                    )
+                at = pl.ds(yy * rows + 16 * band, 16)
+                wmat[group, at, 0:128] = tile(band)
+                wmat[group, at, 128:256] = tile(BANDS + band)
+                wmat[group, at, 256:384] = end[band].astype(BF16)
             return carry
 
         lax.fori_loop(0, SIDE, assemble, 0)
@@ -180,20 +215,40 @@
         if k == 2:
             relays[1].wait_recv()
             relays[3].wait_recv()
+            when_mine(group, relay_ext.wait_recv)
         else:
             along_z[k].wait_recv()
-            half = wbuf.at[group, here, pl.ds(0 if k == 1 else 2, 2)]
-            relays[k] = remote(half, half, e_send.at[k], e_recv.at[k], group_peer(k))
+            when_mine(group, along_z_ext[k].wait_recv)
+            some = wbuf.at[group, here, pl.ds(0, 2) if k == 1 else pl.ds(2, 1)]
+            relays[k] = remote(some, some, e_send.at[k], e_recv.at[k], group_peer(k))
             relays[k].start()
+            if k == 3:
+                when_mine(group, relay_ext.start)
         chunk = wbuf.at[group, here]
+        extra = wext.at[group, y]
 
         def send(i, carry):
             remote(chunk, chunk, b_send.at[k], b_recv.at[k], plane_peer(i)).start()
+            when_mine(group, remote(extra, extra, bx_send.at[k], bx_recv.at[k], plane_peer(i)).start)
             return carry
 
         lax.fori_loop(1, OTHERS + 1, send, 0)
 
+    def wait_group(k):
+        group = (zh + SIDE - k) % SIDE
+        wait_bytes(wbuf.at[0, 0:OTHERS], b_recv.at[k])
+
+        @pl.when(x == group)
+        def _():
+            wait_bytes(wext.at[0, 0 : SIDE - 1], bx_recv.at[k])
+
+        @pl.when(x != group)
+        def _():
+            wait_bytes(wext.at[0], bx_recv.at[k])
+
     relays = {}
+    passed = wext.at[(zh + 1) % SIDE, y]
+    relay_ext = remote(passed, passed, ex_send, ex_recv, group_peer(3))
     for k in (1, 3):
         forward_on(k)
     for c in along_y:
@@ -201,7 +256,7 @@
     forward(zh)
     forward_on(2)
     for k in (1, 3, 2):
-        wait_bytes(wbuf.at[0, 0:OTHERS], b_recv.at[k])
+        wait_group(k)
         forward((zh + SIDE - k) % SIDE)
 
     swap = remote(pred_mine, pred_other, p_send, p_recv, (1 - pair, dp, fsdp))
@@ -231,18 +286,12 @@
         grad = dot(g_pre, normed[...], ((1,), (1,)))
         for_head = dot(hidden[group], g_aug[...], ((1,), (1,)))
         for_head = jnp.where(is_rest, for_head - for_head.astype(BF16).astype(F32), for_head)
-        out = [
-            grad[:, 0:128].astype(BF16),
-            grad[:, 128:256].astype(BF16),
-            (grad[:, 256:384] + for_head).astype(BF16),
-        ]
         for yy in range(SIDE):
-            for band in range(BANDS):
-                for slab in range(SLABS):
-                    q = band * SLABS + slab
-                    top = yy * rows + 16 * band
-                    gsend[group, yy * SIDE + q // SIDE, q % SIDE] = out[slab][top : top + 16, :]
-            gsend[group, yy * SIDE + SIDE - 1, SIDE - 1] = jnp.zeros(TILE, BF16)
+            at = slice(yy * rows, yy * rows + rows)
+            tiles = pack(grad[at, 0:128], grad[at, 128:256], grad[at, 256:384], for_head[at])
+            for t in range(TILES - 1):
+                gsend[group, yy * SIDE + t // SHARE, t % SHARE] = tiles[t]
+            gext[group, yy] = tiles[-1]
 
         def send(i, carry):
             there = ((y + i // SIDE) % SIDE) * SIDE + (x + i % SIDE) % SIDE
@@ -255,57 +304,118 @@
         lax.fori_loop(1, OTHERS + 1, send, 0)
         grecv[group, here] = gsend[group, here]
 
+        def send_ext(b, carry):
+            to = (y + b) % SIDE
+            remote(
+                gext.at[group, to], xrecv.at[here], rx_send.at[group], rx_recv, device(group, to, zh, zl)
+            ).start()
+            return carry
+
+        @pl.when(x == group)
+        def _():
+            lax.fori_loop(1, SIDE, send_ext, 0)
+            xrecv[here] = gext[group, y]
+
+        @pl.when(x != group)
+        def _():
+            lax.fori_loop(0, SIDE, send_ext, 0)
+
     order = [(zh + k) % SIDE for k in (2, 1, 3, 0)]
 
-    def plane_sum(k, group):
+    def plane_sum(group):
         wait_bytes(grecv.at[0, 0:OTHERS], r_recv.at[group])
         total = grecv[group, 0].astype(F32)
         for s in range(1, SIDE * SIDE):
             total = total + grecv[group, s].astype(F32)
         zsend[group] = total
 
-        def send(b, carry):
-            to = (zl + b) % SIDE
-            remote(
-                zsend.at[group, to], zrecv.at[zh * SIDE + zl], z_send, z_recv, device(x, y, group, to)
-            ).start()
-            return carry
-
-        lax.fori_loop(1 if k == 0 else 0, SIDE, send, 0)
+        own_slot = zrecv.at[zh * SIDE + zl]
+
+        def send(to, carry):
+            @pl.when((group != zh) | (to != zl))
+            def _():
+                remote(zsend.at[group, to], own_slot, z_send, z_recv, device(x, y, group, to)).start()
+
+            return carry
+
+        lax.fori_loop(0, SHARE, send, 0)
+
+        @pl.when(x == group)
+        def _():
+            wait_bytes(xrecv.at[0:OTHERS], rx_recv)
+            total = xrecv[0].astype(F32)
+            for s in range(1, SIDE * SIDE):
+                total = total + xrecv[s].astype(F32)
+            zext[...] = total
+
+            @pl.when((group != zh) | (zl != SHARE))
+            def _():
+                remote(zext, own_slot, z_send, z_recv, device(x, y, group, SHARE)).start()
 
     for group in order:
         backward(group)
-    for k, group in zip((2, 1, 3, 0), order):
-        plane_sum(k, group)
-    zrecv[zh * SIDE + zl] = zsend[zh, zl]
-    wait_bytes(zrecv.at[0:OTHERS], z_recv)
-    total = zrecv[0]
-    for s in range(1, SIDE * SIDE):
-        total = total + zrecv[s]
-    own = dp
-    fbuf[own] = total
-
-    def send_piece(i, carry):
-        remote(fbuf.at[own], fbuf.at[own], f_send, f_recv, dp_peer(i)).start()
-        return carry
-
-    lax.fori_loop(1, OTHERS + 1, send_piece, 0)
+    for group in order:
+        plane_sum(group)
+    has_tile = (zl < SHARE) | (x == zh)
+
+    @pl.when(zl < SHARE)
+    def _():
+        zrecv[zh * SIDE + zl] = zsend[zh, zl]
+
+    @pl.when((zl == SHARE) & (x == zh))
+    def _():
+        zrecv[zh * SIDE + zl] = zext[...]
+
+    @pl.when(has_tile)
+    def _():
+        wait_bytes(zrecv.at[0:OTHERS], z_recv)
+        total = zrecv[0]
+        for s in range(1, SIDE * SIDE):
+            total = total + zrecv[s]
+        own = jnp.where(zl < SHARE, x * SHARE + zl, TILES - 1)
+        fbuf[own] = total
+
+        def send_piece(i, carry):
+            remote(fbuf.at[own], fbuf.at[own], f_send, f_recv, dp_peer(i)).start()
+            return carry
+
+        lax.fori_loop(1, OTHERS + 1, send_piece, 0)
 
     for k in (1, 2, 3):
+        group = (zh + SIDE - k) % SIDE
         if k != 2:
             along_z[k].wait_send()
+            when_mine(zh, along_z_ext[k].wait_send)
             relays[k].wait_send()
         wait_bytes(wbuf.at[0, 0:OTHERS], b_send.at[k])
+        when_mine(group, lambda: wait_bytes(xrecv.at[0:OTHERS], bx_send.at[k]))
+    when_mine((zh + 1) % SIDE, relay_ext.wait_send)
     for c in along_y:
         c.wait_send()
     swap.wait_send()
     for group in range(SIDE):
         wait_bytes(gsend.at[0, 0:OTHERS], r_send.at[group])
-    wait_bytes(zrecv.at[0:OTHERS], z_send)
-
-    wait_bytes(fbuf.at[0:OTHERS], f_recv)
+
+        @pl.when(x == group)
+        def _():
+            wait_bytes(gext.at[0, 0 : SIDE - 1], rx_send.at[group])
+
+        @pl.when(x != group)
+        def _():
+            wait_bytes(gext.at[0], rx_send.at[group])
+
+    @pl.when(has_tile)
+    def _():
+        wait_bytes(fbuf.at[0 : TILES - 1], z_send)
+        wait_bytes(fbuf.at[0 : TILES - 1], f_recv)
+        wait_bytes(zrecv.at[0:OTHERS], f_send)
+
+    @pl.when(jnp.logical_not(has_tile))
+    def _():
+        wait_bytes(fbuf, z_send)
+        wait_bytes(fbuf, f_recv)
+
     sums_ref[...] = fbuf[...]
-    wait_bytes(fbuf.at[0:OTHERS], f_send)
 
 
 def results(sums_ref, pred_in_ref, w_rgb_ref, pred_ref, grad_in_ref, grad_down_ref, rgb):
@@ -315,12 +425,13 @@
         for k in range(3):
             at = HEAD + 3 * copy + k
             rgb[at : at + 1, :] = w_rgb_ref[k]
+    end = unpack_last(sums_ref[10], sums_ref[11], sums_ref[12])
     for band in range(BANDS):
         at = slice(16 * band, 16 * band + 16)
-        grad_in_ref[at, 0:128] = sums_ref[band * SLABS]
-        grad_in_ref[at, 128:256] = sums_ref[band * SLABS + 1]
-        grad_in_ref[at, 256:320] = sums_ref[band * SLABS + 2][:, 0:64]
-    last = jnp.concatenate([sums_ref[band * SLABS + 2] for band in range(BANDS)], axis=0)
+        grad_in_ref[at, 0:128] = sums_ref[band]
+        grad_in_ref[at, 128:256] = sums_ref[BANDS + band]
+        grad_in_ref[at, 256:320] = end[band][:, 0:64]
+    last = jnp.concatenate(end, axis=0)
     grad_down_ref[...] = dot(last, rgb[...], ((1,), (0,)), precision=HIGH)
 
 
@@ -338,14 +449,15 @@
         lambda *refs: kernel(loss_scale, *refs),
         out_shape=(
             jax.ShapeDtypeStruct((3, 1, pixels), F32),
-            jax.ShapeDtypeStruct((plane, *TILE), F32),
+            jax.ShapeDtypeStruct((TILES, *TILE), F32),
         ),
         in_specs=[vmem] * 8,
         out_specs=(vmem, vmem),
         scratch_shapes=[
             pltpu.VMEM((128, channels), F32),
             pltpu.VMEM((384, pixels), BF16),
-            pltpu.VMEM((SIDE, plane, SIDE, *TILE), BF16),
+            pltpu.VMEM((SIDE, plane, SHARE, *TILE), BF16),
+            pltpu.VMEM((SIDE, SIDE, *TILE), BF16),
             pltpu.VMEM((SIDE, group_rows, 384), BF16),
             pltpu.VMEM((SIDE, 16, group_rows), BF16),
             pltpu.VMEM((SIDE, group_rows, pixels), BF16),
@@ -354,11 +466,15 @@
             pltpu.VMEM((8, pixels), F32),
             pltpu.VMEM((16, pixels), F32),
             pltpu.VMEM((128, pixels), BF16),
-            pltpu.VMEM((SIDE, plane, SIDE, *TILE), BF16),
-            pltpu.VMEM((SIDE, plane, SIDE, *TILE), BF16),
-            pltpu.VMEM((SIDE, SIDE, *TILE), F32),
+            pltpu.VMEM((SIDE, plane, SHARE, *TILE), BF16),
+            pltpu.VMEM((SIDE, SIDE, *TILE), BF16),
+            pltpu.VMEM((SIDE, plane, SHARE, *TILE), BF16),
+            pltpu.VMEM((plane, *TILE), BF16),
+            pltpu.VMEM((SIDE, SHARE, *TILE), F32),
+            pltpu.VMEM(TILE, F32),
             pltpu.VMEM((plane, *TILE), F32),
-            pltpu.VMEM((plane, *TILE), F32),
+            pltpu.VMEM((TILES, *TILE), F32),
+            dma((SIDE,)), dma((SIDE,)), dma, dma, dma((SIDE,)), dma((SIDE,)), dma((SIDE,)), dma((SIDE,)), dma((SIDE,)), dma,
             dma((SIDE,)), dma((SIDE,)), dma((SIDE,)), dma((SIDE,)),
             dma((SIDE,)), dma((SIDE,)), dma((SIDE,)), dma((SIDE,)), dma, dma,
             dma((SIDE,)), dma((SIDE,)), dma, dma, dma, dma,

time: 61.8 us -> 59.6 us (0.964)
  Pallas kernels: 61 us -> 58.4 us
    pallas_call x1, Pallas kernels: 59.1 us -> 56.5 us  [on_device(): pl.pallas_call(lambda *refs: kernel(loss_scale, *refs), out_shape=(jax.Sh...]
where the time goes in v4:
time: 59.6 us; the launch traced here: 59.1 us
  Pallas kernels  58.4 us (98%)
  between operations  0.64 us (1%)
    pallas_call x1, Pallas kernels, on_device(): pl.pallas_call(lambda *refs: kernel(loss_scale, *refs), out_shape=(jax.Sh...  56.5 us
    pallas_call x1, Pallas kernels, on_device(): pl.pallas_call(results, out_shape=(jax.ShapeDtypeStruct((3, 1, pixels), F...  1.88 us

profile of v4, /device:TPU:1, one launch (start us, length us, event | category | flops | bytes accessed | tf_op | source)
XLA Modules:
  0.0 59.1 jit_solution(9038593337068997188)
XLA Ops:
  0.6 56.5 %shard_map.103 = (f32[3,1,1024]{2,1,0:T(1,128)}, f32[13,16,128]{2,1,0:T(8,128)}) custom-call(bf16[320,1024]{1,0:T(8,128)(2,1)} %bitcast.11, f32[64,320]{1,0:T(8,128)} %refs_1_.1, s32[1,64]{1,0:T(1,128)} %bitcast.18, bf16[80,320]{1,0:T(8,128)(2,1)} %bitcast.14, bf16[80,320]{1,0:T(8,128)(2,1)} %bitcast.15, f32[3,1,320]{2,1,0:T(1,128)} %bitcast.9, ...), custom_call_target="tpu_custom_call" | custom-call | flops 3019898880 | bytes 2097152 | tf_op jit(solution)/shard_map/pallas_call | solution.py:448
  57.2 1.9 %shard_map.104 = (f32[3,1,1024]{2,1,0:T(1,128)}, f32[80,320]{1,0:T(8,128)}, f32[80,320]{1,0:T(8,128)}) custom-call(f32[13,16,128]{2,1,0:T(8,128)} %get-tuple-element.8.sums_ref, f32[3,1,1024]{2,1,0:T(1,128)} %get-tuple-element.9.pred_in_ref, f32[3,1,320]{2,1,0:T(1,128)} %bitcast.10), custom_call_target="tpu_custom_call" | custom-call | tf_op jit(solution)/shard_map/pallas_call | solution.py:487

commit v5 on v4

--- a/solution.py
+++ b/solution.py
@@ -26,15 +26,20 @@
 TILES = SIDE * SHARE + 1
 
 
-def pack(slab0, slab1, last, head):
+def pack(slab0, slab1, last):
     band = [slice(16 * b, 16 * b + 16) for b in range(BANDS)]
     tiles = [slab0[at] for at in band] + [slab1[at] for at in band]
     tiles.append(last[band[0]] + pltpu.roll(last[band[1]], 64, 1))
     tiles.append(last[band[2]] + pltpu.roll(last[band[3]], 64, 1))
+    return [t.astype(BF16) for t in tiles]
+
+
+def pack_end(last, head):
+    band = [slice(16 * b, 16 * b + 16) for b in range(BANDS)]
     end = last[band[4]] + head[band[0]]
     for b in range(1, BANDS):
         end = end + pltpu.roll(head[band[b]], PARTS * b, 1)
-    return [t.astype(BF16) for t in tiles] + [end.astype(BF16)]
+    return end.astype(BF16)
 
 
 def unpack_last(ten, eleven, end):
@@ -50,9 +55,10 @@
 
 def kernel(
     loss_scale,
-    x_ref, table_ref, levels_ref, w_in_ref, w_down_ref, w_rgb_ref, target_ref, counts_ref,
+    x_hbm, table_hbm, w_in_hbm, w_down_hbm, levels_ref, w_rgb_ref, target_ref, counts_ref,
     pred_ref, sums_ref,
-    rgb, normed, wbuf, wext, wmat, head_t, hidden, slope, pred_mine, pred_other, g_rows, g_aug,
+    x_ref, table_ref, w_in_ref, w_down_ref, in_sem,
+    rgb_rows, rgb_parts, normed, wbuf, wext, wmat, head_t, hidden, slope, pred_mine, pred_other, g_rows, g_aug,
     gsend, gext, grecv, xrecv, zsend, zext, zrecv, fbuf,
     ax_send, ax_recv, ex_send, ex_recv, yx_send, yx_recv, bx_send, bx_recv, rx_send, rx_recv,
     a_send, a_recv, e_send, e_recv, y_send, y_recv, b_send, b_recv, p_send, p_recv,
@@ -64,8 +70,7 @@
     x, zl = dp // SIDE, dp % SIDE
     y, zh = fsdp // SIDE, fsdp % SIDE
     here = y * SIDE + x
-    pixels = x_ref.shape[1]
-    channels = x_ref.shape[0]
+    channels, pixels = x_ref.shape
     rows = w_in_ref.shape[0]
 
     def device(x_, y_, zh_, zl_):
@@ -82,6 +87,13 @@
 
     def group_peer(k):
         return device(x, y, (zh + k) % SIDE, zl)
+
+    loads = {}
+    for n, (src, dst) in enumerate(
+        ((w_in_hbm, w_in_ref), (w_down_hbm, w_down_ref), (x_hbm, x_ref), (table_hbm, table_ref))
+    ):
+        loads[n] = pltpu.make_async_copy(src, dst, in_sem.at[n])
+        loads[n].start()
 
     barrier = pltpu.get_barrier_semaphore()
 
@@ -100,23 +112,13 @@
         greet(group_peer(k))
     greet((1 - pair, dp, fsdp))
 
-    rgb[...] = jnp.zeros_like(rgb)
-    for copy in range(3):
-        for k in range(3):
-            at = HEAD + 3 * copy + k
-            rgb[at : at + 1, :] = w_rgb_ref[k]
-    lane = lax.broadcasted_iota(jnp.int32, (rows, 128), 1)
-    head = dot(w_down_ref[...].astype(F32), rgb[...], ((1,), (1,)), precision=HIGH)
-    head_hi = head.astype(BF16).astype(F32)
-    is_lo = (lane >= HEAD + 3) & (lane < HEAD + 6)
-    head = jnp.where(is_lo, head - head_hi, head_hi)
+    loads[0].wait()
     w_own = w_in_ref[...]
     last = w_own[:, 256:320].astype(F32)
     last = jnp.concatenate([last, jnp.zeros((rows, 64), F32)], axis=1)
-    tiles = pack(w_own[:, 0:128], w_own[:, 128:256], last, head)
+    tiles = pack(w_own[:, 0:128], w_own[:, 128:256], last)
     for t in range(TILES - 1):
         wbuf[zh, y * SIDE + t // SHARE, t % SHARE] = tiles[t]
-    wext[zh, y] = tiles[-1]
 
     pl.semaphore_wait(barrier, OTHERS + 12 + 2 + 1)
 
@@ -140,21 +142,47 @@
         def _():
             copy()
 
-    along_z_ext = {}
-    for k in (1, 3):
-        along_z_ext[k] = remote(wext.at[zh, y], wext.at[zh, y], ax_send.at[k], ax_recv.at[k], group_peer(k))
-        when_mine(zh, along_z_ext[k].start)
     block = wbuf.at[zh, pl.ds(y * SIDE, SIDE)]
     along_y = []
     for m in range(1, SIDE):
         c = remote(block, block, y_send.at[m], y_recv.at[m], device(x, (y + m) % SIDE, zh, zl))
         c.start()
         along_y.append(c)
+
+    rgb_rows[...] = jnp.zeros_like(rgb_rows)
+    for copy in range(3):
+        for k in range(3):
+            at = 3 * copy + k
+            rgb_rows[at : at + 1, :] = w_rgb_ref[k]
+    part = rgb_rows[...]
+    part_hi = part.astype(BF16).astype(F32)
+    part_mid = (part - part_hi).astype(BF16).astype(F32)
+    part_lo = part - part_hi - part_mid
+    rgb_parts[...] = jnp.zeros_like(rgb_parts)
+    for n, p in enumerate((part_hi, part_mid, part_lo)):
+        rgb_parts[HEAD + 16 * n : HEAD + 16 * n + 16, :] = p.astype(BF16)
+    loads[1].wait()
+    head = dot(w_down_ref[...], rgb_parts[...], ((1,), (1,)))
+    head = head + pltpu.roll(head, 112, 1) + pltpu.roll(head, 96, 1)
+    lane = lax.broadcasted_iota(jnp.int32, (rows, 128), 1)
+    head = jnp.where((lane >= HEAD) & (lane < HEAD + PARTS), head, 0.0)
+    head_hi = head.astype(BF16).astype(F32)
+    is_lo = (lane >= HEAD + 3) & (lane < HEAD + 6)
+    head = jnp.where(is_lo, head - head_hi, head_hi)
+    own_ext = wext.at[zh, y]
+    own_ext[...] = pack_end(last, head)
+    along_z_ext = {}
+    for k in (1, 3):
+        along_z_ext[k] = remote(own_ext, own_ext, ax_send.at[k], ax_recv.at[k], group_peer(k))
+        when_mine(zh, along_z_ext[k].start)
+    for m in range(1, SIDE):
         peer = device(x, (y + m) % SIDE, zh, zl)
-        c = remote(wext.at[zh, y], wext.at[zh, y], yx_send.at[m], yx_recv.at[m], peer)
+        c = remote(own_ext, own_ext, yx_send.at[m], yx_recv.at[m], peer)
         c.start()
         along_y.append(c)
 
+    loads[2].wait()
+    loads[3].wait()
     image = ((dp * SIDE * SIDE + fsdp) * pixels) // IMG_PIX
     levels = levels_ref[...].astype(F32)
     spots = lax.broadcasted_iota(jnp.int32, levels.shape, 1)
@@ -168,10 +196,6 @@
     normed[0:channels, :] = (xf * lax.rsqrt(mean_sq + EPS) * gain).astype(BF16)
     normed[channels:, :] = jnp.zeros((384 - channels, pixels), BF16)
 
-    part = rgb[HEAD : HEAD + 16, :]
-    part_hi = part.astype(BF16).astype(F32)
-    part_mid = (part - part_hi).astype(BF16).astype(F32)
-    part_lo = part - part_hi - part_mid
     row = lax.broadcasted_iota(jnp.int32, part.shape, 0)
     part = jnp.where(row < 3, part_hi, jnp.where(row < 6, part_mid, part_lo)).astype(BF16)
     direct = dot(part, x_ref[...], ((1,), (0,)))
@@ -180,7 +204,7 @@
 
     wide = 256
 
-    def forward(group):
+    def forward(group, now=True):
         def assemble(yy, carry):
             def tile(t):
                 return wbuf[group, yy * SIDE + t // SHARE, t % SHARE]
@@ -203,7 +227,7 @@
             act = pre * sig
             hid = act.astype(BF16)
             hidden[group, :, at] = hid
-            slope[group, :, at] = sig + act * (1.0 - sig)
+            slope[group, :, at] = sig + act * (1.0 - sig) if now else pre
             through = dot(head_t[group], hid, ((1,), (0,)))
             pred_mine[0:3, at] += through[0:3] + through[3:6]
             return carry
@@ -255,53 +279,75 @@
         c.wait_recv()
     forward(zh)
     forward_on(2)
+    samples = counts_ref[...].astype(F32)
+    weight = samples / (samples + 64.0)
+    g_rows[...] = jnp.zeros_like(g_rows)
+    g_aug[...] = jnp.zeros_like(g_aug)
     for k in (1, 3, 2):
         wait_group(k)
-        forward((zh + SIDE - k) % SIDE)
+        forward((zh + SIDE - k) % SIDE, now=k != 2)
 
     swap = remote(pred_mine, pred_other, p_send, p_recv, (1 - pair, dp, fsdp))
     swap.start()
     pred = pred_mine[0:3, :]
     for k in range(3):
         pred_ref[k] = pred[k : k + 1]
-    samples = counts_ref[...].astype(F32)
-    weight = samples / (samples + 64.0)
     toward = weight * (pred - target_ref[...])
+
+    far = (zh + 2) % SIDE
+
+    def make_slope(n, carry):
+        at = pl.ds(pl.multiple_of(n * wide, wide), wide)
+        pre = slope[far, :, at]
+        sig = 0.5 * jnp.tanh(0.5 * pre) + 0.5
+        slope[far, :, at] = sig + pre * sig * (1.0 - sig)
+        return carry
+
+    lax.fori_loop(0, pixels // wide, make_slope, 0)
     swap.wait_recv()
     g_pred = (toward + DISTILL * (pred - pred_other[0:3, :])) * loss_scale
     g_hi = g_pred.astype(BF16).astype(F32)
-    g_rows[...] = jnp.zeros_like(g_rows)
     g_rows[0:3, :] = g_hi
     g_rows[3:6, :] = g_hi
     g_rows[6:9, :] = g_pred - g_hi
-    g_aug[...] = jnp.zeros_like(g_aug)
     g_aug[HEAD : HEAD + 16, :] = g_rows[...].astype(BF16)
 
-    lane_g = lax.broadcasted_iota(jnp.int32, (SIDE * rows, 128), 1)
-    is_rest = (lane_g >= HEAD + 3) & (lane_g < HEAD + 6)
-
-    def backward(group):
-        g_hidden = dot(wmat[group, :, 256:384], g_aug[...], ((1,), (0,)))
-        g_pre = (g_hidden * slope[group]).astype(BF16)
+    def backward_rows(group, picks):
+        ys = [(y + b) % SIDE for b in picks]
+
+        def pick(ref, *rest):
+            return jnp.concatenate([ref[(group, pl.ds(yy * rows, rows), *rest)] for yy in ys], axis=0)
+
+        g_hidden = dot(pick(wmat, slice(256, 384)), g_aug[...], ((1,), (0,)))
+        g_pre = (g_hidden * pick(slope, slice(None))).astype(BF16)
         grad = dot(g_pre, normed[...], ((1,), (1,)))
-        for_head = dot(hidden[group], g_aug[...], ((1,), (1,)))
+        for_head = dot(pick(hidden, slice(None)), g_aug[...], ((1,), (1,)))
+        lane_g = lax.broadcasted_iota(jnp.int32, for_head.shape, 1)
+        is_rest = (lane_g >= HEAD + 3) & (lane_g < HEAD + 6)
         for_head = jnp.where(is_rest, for_head - for_head.astype(BF16).astype(F32), for_head)
-        for yy in range(SIDE):
-            at = slice(yy * rows, yy * rows + rows)
-            tiles = pack(grad[at, 0:128], grad[at, 128:256], grad[at, 256:384], for_head[at])
+        for n, yy in enumerate(ys):
+            at = slice(n * rows, n * rows + rows)
+            tiles = pack(grad[at, 0:128], grad[at, 128:256], grad[at, 256:384])
             for t in range(TILES - 1):
                 gsend[group, yy * SIDE + t // SHARE, t % SHARE] = tiles[t]
-            gext[group, yy] = tiles[-1]
-
-        def send(i, carry):
-            there = ((y + i // SIDE) % SIDE) * SIDE + (x + i % SIDE) % SIDE
-            remote(
-                gsend.at[group, there], grecv.at[group, here],
-                r_send.at[group], r_recv.at[group], plane_peer(i),
-            ).start()
-            return carry
-
-        lax.fori_loop(1, OTHERS + 1, send, 0)
+            gext[group, yy] = pack_end(grad[at, 256:384], for_head[at])
+
+        for b in picks:
+            yy = (y + b) % SIDE
+
+            def send(a, carry):
+                xx = (x + a) % SIDE
+                remote(
+                    gsend.at[group, yy * SIDE + xx], grecv.at[group, here],
+                    r_send.at[group], r_recv.at[group], device(xx, yy, zh, zl),
+                ).start()
+                return carry
+
+            lax.fori_loop(1 if b == 0 else 0, SIDE, send, 0)
+
+    def backward(group, parts):
+        for picks in parts:
+            backward_rows(group, picks)
         grecv[group, here] = gsend[group, here]
 
         def send_ext(b, carry):
@@ -352,8 +398,9 @@
             def _():
                 remote(zext, own_slot, z_send, z_recv, device(x, y, group, SHARE)).start()
 
-    for group in order:
-        backward(group)
+    whole = (2, 1, 3, 0)
+    for n, group in enumerate(order):
+        backward(group, (whole[:2], whole[2:]) if n == 0 else (whole,))
     for group in order:
         plane_sum(group)
     has_tile = (zl < SHARE) | (x == zh)
@@ -418,21 +465,19 @@
     sums_ref[...] = fbuf[...]
 
 
-def results(sums_ref, pred_in_ref, w_rgb_ref, pred_ref, grad_in_ref, grad_down_ref, rgb):
+def results(sums_ref, pred_in_ref, w_rgb_ref, pred_ref, grad_in_ref, grad_down_ref):
     pred_ref[...] = pred_in_ref[...]
-    rgb[...] = jnp.zeros_like(rgb)
-    for copy in range(3):
-        for k in range(3):
-            at = HEAD + 3 * copy + k
-            rgb[at : at + 1, :] = w_rgb_ref[k]
     end = unpack_last(sums_ref[10], sums_ref[11], sums_ref[12])
     for band in range(BANDS):
         at = slice(16 * band, 16 * band + 16)
         grad_in_ref[at, 0:128] = sums_ref[band]
         grad_in_ref[at, 128:256] = sums_ref[BANDS + band]
         grad_in_ref[at, 256:320] = end[band][:, 0:64]
-    last = jnp.concatenate(end, axis=0)
-    grad_down_ref[...] = dot(last, rgb[...], ((1,), (0,)), precision=HIGH)
+        total = 0.0
+        for k in range(3):
+            weight = sum(end[band][:, at + k : at + k + 1] for at in range(HEAD, HEAD + PARTS, 3))
+            total = total + weight * w_rgb_ref[k]
+        grad_down_ref[16 * band : 16 * band + 16, :] = total
 
 
 def on_device(loss_scale, features, level_gain, levels, w_in, w_down, w_rgb, target, counts):
@@ -451,10 +496,16 @@
             jax.ShapeDtypeStruct((3, 1, pixels), F32),
             jax.ShapeDtypeStruct((TILES, *TILE), F32),
         ),
-        in_specs=[vmem] * 8,
+        in_specs=[pl.BlockSpec(memory_space=pl.ANY)] * 4 + [vmem] * 4,
         out_specs=(vmem, vmem),
         scratch_shapes=[
-            pltpu.VMEM((128, channels), F32),
+            pltpu.VMEM((channels, pixels), BF16),
+            pltpu.VMEM(level_gain.shape, F32),
+            pltpu.VMEM((rows, channels), BF16),
+            pltpu.VMEM((rows, channels), BF16),
+            dma((4,)),
+            pltpu.VMEM((16, channels), F32),
+            pltpu.VMEM((128, channels), BF16),
             pltpu.VMEM((384, pixels), BF16),
             pltpu.VMEM((SIDE, plane, SHARE, *TILE), BF16),
             pltpu.VMEM((SIDE, SIDE, *TILE), BF16),
@@ -483,7 +534,7 @@
             collective_id=0, has_side_effects=True, vmem_limit_bytes=56 * 2**20
         ),
         cost_estimate=pl.CostEstimate(flops=flops, bytes_accessed=2**21, transcendentals=all_rows * pixels),
-    )(features[0], level_gain, levels[None], w_in[0], w_down[0], colours, target, counts[None])
+    )(features[0], level_gain, w_in[0], w_down[0], levels[None], colours, target, counts[None])
     pred, grad_in, grad_down = pl.pallas_call(
         results,
         out_shape=(
@@ -493,7 +544,6 @@
         ),
         in_specs=[vmem] * 3,
         out_specs=(vmem, vmem, vmem),
-        scratch_shapes=[pltpu.VMEM((128, channels), F32)],
     )(sums, pred, colours)
     return jnp.transpose(pred, (1, 0, 2)), grad_in[None], grad_down[None]
 

time: 59.6 us -> 58.9 us (0.988)
  Pallas kernels: 58.4 us -> 57.5 us
    pallas_call x1, Pallas kernels: 56.5 us -> 55.6 us  [on_device(): pl.pallas_call(lambda *refs: kernel(loss_scale, *refs), out_shape=(jax.Sh...]
where the time goes in v5:
time: 58.9 us; the launch traced here: 58.1 us
  Pallas kernels  57.5 us (98%)
  between operations  0.64 us (1%)
    pallas_call x1, Pallas kernels, on_device(): pl.pallas_call(lambda *refs: kernel(loss_scale, *refs), out_shape=(jax.Sh...  55.6 us
    pallas_call x1, Pallas kernels, on_device(): pl.pallas_call(results, out_shape=(jax.ShapeDtypeStruct((3, 1, pixels), F...  1.82 us

profile of v5, /device:TPU:1, one launch (start us, length us, event | category | flops | bytes accessed | tf_op | source)
XLA Modules:
  0.0 58.1 jit_solution(13185660363635697832)
XLA Ops:
  0.6 55.6 %shard_map.103 = (f32[3,1,1024]{2,1,0:T(1,128)}, f32[13,16,128]{2,1,0:T(8,128)}) custom-call(bf16[320,1024]{1,0:T(8,128)(2,1)} %bitcast.11, f32[64,320]{1,0:T(8,128)} %refs_1_.1, bf16[80,320]{1,0:T(8,128)(2,1)} %bitcast.14, bf16[80,320]{1,0:T(8,128)(2,1)} %bitcast.15, s32[1,64]{1,0:T(1,128)} %bitcast.18, f32[3,1,320]{2,1,0:T(1,128)} %bitcast.9, ...), custom_call_target="tpu_custom_call" | custom-call | flops 3019898880 | bytes 2097152 | tf_op jit(solution)/shard_map/pallas_call | solution.py:493
  56.3 1.8 %shard_map.104 = (f32[3,1,1024]{2,1,0:T(1,128)}, f32[80,320]{1,0:T(8,128)}, f32[80,320]{1,0:T(8,128)}) custom-call(f32[13,16,128]{2,1,0:T(8,128)} %get-tuple-element.8.sums_ref, f32[3,1,1024]{2,1,0:T(1,128)} %get-tuple-element.9.pred_in_ref, f32[3,1,320]{2,1,0:T(1,128)} %bitcast.10), custom_call_target="tpu_custom_call" | custom-call | tf_op jit(solution)/shard_map/pallas_call | solution.py:538

commit v6 on v5

--- a/solution.py
+++ b/solution.py
@@ -58,10 +58,10 @@
     x_hbm, table_hbm, w_in_hbm, w_down_hbm, levels_ref, w_rgb_ref, target_ref, counts_ref,
     pred_ref, sums_ref,
     x_ref, table_ref, w_in_ref, w_down_ref, in_sem,
-    rgb_rows, rgb_parts, normed, wbuf, wext, wmat, head_t, hidden, slope, pred_mine, pred_other, g_rows, g_aug,
+    rgb_rows, rgb_parts, normed, wbuf, wext, wmat, normed_t, hidden, slope, pred_mine, pred_other, g_rows, g_aug,
     gsend, gext, grecv, xrecv, zsend, zext, zrecv, fbuf,
     ax_send, ax_recv, ex_send, ex_recv, yx_send, yx_recv, bx_send, bx_recv, rx_send, rx_recv,
-    a_send, a_recv, e_send, e_recv, y_send, y_recv, b_send, b_recv, p_send, p_recv,
+    a_send, a_recv, e_send, e_recv, y_send, y_recv, b_send, b_recv, c_recv, cx_recv, p_send, p_recv,
     r_send, r_recv, z_send, z_recv, f_send, f_recv,
 ):
     pair = lax.axis_index("pair")
@@ -193,8 +193,10 @@
     gain = jnp.broadcast_to(gain, (128, 384)).T[:channels, 0:1]
     xf = x_ref[...].astype(F32)
     mean_sq = jnp.mean(xf * xf, axis=0, keepdims=True)
-    normed[0:channels, :] = (xf * lax.rsqrt(mean_sq + EPS) * gain).astype(BF16)
-    normed[channels:, :] = jnp.zeros((384 - channels, pixels), BF16)
+    whole = xf * lax.rsqrt(mean_sq + EPS) * gain
+    whole = jnp.concatenate([whole, jnp.zeros((384 - channels, pixels), F32)], axis=0)
+    normed[...] = whole.astype(BF16)
+    normed_t[...] = whole.T.astype(BF16)
 
     row = lax.broadcasted_iota(jnp.int32, part.shape, 0)
     part = jnp.where(row < 3, part_hi, jnp.where(row < 6, part_mid, part_lo)).astype(BF16)
@@ -204,50 +206,67 @@
 
     wide = 256
 
-    def forward(group, now=True):
-        def assemble(yy, carry):
-            def tile(t):
-                return wbuf[group, yy * SIDE + t // SHARE, t % SHARE]
-
-            end = unpack_last(tile(10).astype(F32), tile(11).astype(F32), wext[group, yy].astype(F32))
-            for band in range(BANDS):
-                at = pl.ds(yy * rows + 16 * band, 16)
-                wmat[group, at, 0:128] = tile(band)
-                wmat[group, at, 128:256] = tile(BANDS + band)
-                wmat[group, at, 256:384] = end[band].astype(BF16)
+    def assemble(group, yy):
+        def tile(t):
+            return wbuf[group, yy * SIDE + t // SHARE, t % SHARE]
+
+        end = unpack_last(tile(10).astype(F32), tile(11).astype(F32), wext[group, yy].astype(F32))
+        for band in range(BANDS):
+            at = pl.ds(yy * rows + 16 * band, 16)
+            wmat[group, at, 0:128] = tile(band)
+            wmat[group, at, 128:256] = tile(BANDS + band)
+            wmat[group, at, 256:384] = end[band].astype(BF16)
+
+    def sigmoid(pre):
+        return 0.5 * jnp.tanh(0.5 * pre) + 0.5
+
+    def forward(group):
+        def assemble_one(yy, carry):
+            assemble(group, yy)
             return carry
 
-        lax.fori_loop(0, SIDE, assemble, 0)
-        head_t[group] = wmat[group, :, 256:384].astype(F32).T[HEAD : HEAD + 16].astype(BF16)
-
-        def columns(n, carry):
-            at = pl.ds(pl.multiple_of(n * wide, wide), wide)
+        lax.fori_loop(0, SIDE, assemble_one, 0)
+        head_t = wmat[group, :, 256:384].astype(F32).T[HEAD : HEAD + 16].astype(BF16)
+        for n in range(pixels // wide):
+            at = slice(n * wide, n * wide + wide)
             pre = dot(wmat[group], normed[:, at], ((1,), (0,)))
-            sig = 0.5 * jnp.tanh(0.5 * pre) + 0.5
+            sig = sigmoid(pre)
             act = pre * sig
             hid = act.astype(BF16)
             hidden[group, :, at] = hid
-            slope[group, :, at] = sig + act * (1.0 - sig) if now else pre
-            through = dot(head_t[group], hid, ((1,), (0,)))
+            slope[group, :, at] = sig + act * (1.0 - sig)
+            through = dot(head_t, hid, ((1,), (0,)))
             pred_mine[0:3, at] += through[0:3] + through[3:6]
-            return carry
-
-        lax.fori_loop(0, pixels // wide, columns, 0, unroll=True)
+
+    def forward_far(yy):
+        assemble(far, yy)
+        mine = pl.ds(yy * rows, rows)
+        head_t = wmat[far, mine, 256:384].astype(F32).T[HEAD : HEAD + 16].astype(BF16)
+        for n in range(pixels // wide):
+            at = slice(n * wide, n * wide + wide)
+            pre = dot(wmat[far, mine, :], normed[:, at], ((1,), (0,)))
+            slope[far, mine, at] = pre
+            hid = (pre * sigmoid(pre)).astype(BF16)
+            hidden[far, mine, at] = hid
+            through = dot(head_t, hid, ((1,), (0,)))
+            pred_mine[0:3, at] += through[0:3] + through[3:6]
+
+    relays = {}
+    passed = wext.at[(zh + 1) % SIDE, y]
+    relay_ext = remote(passed, passed, ex_send, ex_recv, group_peer(3))
+
+    def relay(k):
+        group = (zh + SIDE - k) % SIDE
+        along_z[k].wait_recv()
+        some = wbuf.at[group, here, pl.ds(0, 2) if k == 1 else pl.ds(2, 1)]
+        relays[k] = remote(some, some, e_send.at[k], e_recv.at[k], group_peer(k))
+        relays[k].start()
+        when_mine(group, along_z_ext[k].wait_recv)
+        if k == 3:
+            when_mine(group, relay_ext.start)
 
     def forward_on(k):
         group = (zh + SIDE - k) % SIDE
-        if k == 2:
-            relays[1].wait_recv()
-            relays[3].wait_recv()
-            when_mine(group, relay_ext.wait_recv)
-        else:
-            along_z[k].wait_recv()
-            when_mine(group, along_z_ext[k].wait_recv)
-            some = wbuf.at[group, here, pl.ds(0, 2) if k == 1 else pl.ds(2, 1)]
-            relays[k] = remote(some, some, e_send.at[k], e_recv.at[k], group_peer(k))
-            relays[k].start()
-            if k == 3:
-                when_mine(group, relay_ext.start)
         chunk = wbuf.at[group, here]
         extra = wext.at[group, y]
 
@@ -258,6 +277,36 @@
 
         lax.fori_loop(1, OTHERS + 1, send, 0)
 
+    far = (zh + 2) % SIDE
+    y_steps = (0, 1, 3, 2)
+
+    def forward_far_on():
+        relays[1].wait_recv()
+        relays[3].wait_recv()
+        when_mine(far, relay_ext.wait_recv)
+        chunk = wbuf.at[far, here]
+        extra = wext.at[far, y]
+        for b in y_steps:
+
+            def send(a, carry):
+                peer = device((x + a) % SIDE, (y + b) % SIDE, zh, zl)
+                remote(chunk, chunk, b_send.at[2], c_recv.at[b], peer).start()
+                when_mine(far, remote(extra, extra, bx_send.at[2], cx_recv.at[b], peer).start)
+                return carry
+
+            lax.fori_loop(1 if b == 0 else 0, SIDE, send, 0)
+
+    def wait_far(b):
+        if b == 0:
+            wait_bytes(wbuf.at[0, 0 : SIDE - 1], c_recv.at[b])
+
+            @pl.when(x != far)
+            def _():
+                wait_bytes(wext.at[0, 0], cx_recv.at[b])
+        else:
+            wait_bytes(wbuf.at[0, 0:SIDE], c_recv.at[b])
+            wait_bytes(wext.at[0, 0], cx_recv.at[b])
+
     def wait_group(k):
         group = (zh + SIDE - k) % SIDE
         wait_bytes(wbuf.at[0, 0:OTHERS], b_recv.at[k])
@@ -270,22 +319,24 @@
         def _():
             wait_bytes(wext.at[0], bx_recv.at[k])
 
-    relays = {}
-    passed = wext.at[(zh + 1) % SIDE, y]
-    relay_ext = remote(passed, passed, ex_send, ex_recv, group_peer(3))
+    for k in (1, 3):
+        relay(k)
     for k in (1, 3):
         forward_on(k)
     for c in along_y:
         c.wait_recv()
     forward(zh)
-    forward_on(2)
+    forward_far_on()
     samples = counts_ref[...].astype(F32)
     weight = samples / (samples + 64.0)
     g_rows[...] = jnp.zeros_like(g_rows)
     g_aug[...] = jnp.zeros_like(g_aug)
-    for k in (1, 3, 2):
+    for k in (1, 3):
         wait_group(k)
-        forward((zh + SIDE - k) % SIDE, now=k != 2)
+        forward((zh + SIDE - k) % SIDE)
+    for b in y_steps:
+        wait_far(b)
+        forward_far((y + SIDE - b) % SIDE)
 
     swap = remote(pred_mine, pred_other, p_send, p_recv, (1 - pair, dp, fsdp))
     swap.start()
@@ -294,12 +345,10 @@
         pred_ref[k] = pred[k : k + 1]
     toward = weight * (pred - target_ref[...])
 
-    far = (zh + 2) % SIDE
-
     def make_slope(n, carry):
         at = pl.ds(pl.multiple_of(n * wide, wide), wide)
         pre = slope[far, :, at]
-        sig = 0.5 * jnp.tanh(0.5 * pre) + 0.5
+        sig = sigmoid(pre)
         slope[far, :, at] = sig + pre * sig * (1.0 - sig)
         return carry
 
@@ -320,7 +369,7 @@
 
         g_hidden = dot(pick(wmat, slice(256, 384)), g_aug[...], ((1,), (0,)))
         g_pre = (g_hidden * pick(slope, slice(None))).astype(BF16)
-        grad = dot(g_pre, normed[...], ((1,), (1,)))
+        grad = dot(g_pre, normed_t[...], ((1,), (0,)))
         for_head = dot(pick(hidden, slice(None)), g_aug[...], ((1,), (1,)))
         lane_g = lax.broadcasted_iota(jnp.int32, for_head.shape, 1)
         is_rest = (lane_g >= HEAD + 3) & (lane_g < HEAD + 6)
@@ -398,9 +447,8 @@
             def _():
                 remote(zext, own_slot, z_send, z_recv, device(x, y, group, SHARE)).start()
 
-    whole = (2, 1, 3, 0)
     for n, group in enumerate(order):
-        backward(group, (whole[:2], whole[2:]) if n == 0 else (whole,))
+        backward(group, ((2,), (1,), (3, 0)) if n == 0 else ((2, 1, 3, 0),))
     for group in order:
         plane_sum(group)
     has_tile = (zl < SHARE) | (x == zh)
@@ -493,8 +541,8 @@
     pred, sums = pl.pallas_call(
         lambda *refs: kernel(loss_scale, *refs),
         out_shape=(
-            jax.ShapeDtypeStruct((3, 1, pixels), F32),
-            jax.ShapeDtypeStruct((TILES, *TILE), F32),
+            pltpu.VMEM((3, 1, pixels), F32),
+            pltpu.VMEM((TILES, *TILE), F32),
         ),
         in_specs=[pl.BlockSpec(memory_space=pl.ANY)] * 4 + [vmem] * 4,
         out_specs=(vmem, vmem),
@@ -510,7 +558,7 @@
             pltpu.VMEM((SIDE, plane, SHARE, *TILE), BF16),
             pltpu.VMEM((SIDE, SIDE, *TILE), BF16),
             pltpu.VMEM((SIDE, group_rows, 384), BF16),
-            pltpu.VMEM((SIDE, 16, group_rows), BF16),
+            pltpu.VMEM((pixels, 384), BF16),
             pltpu.VMEM((SIDE, group_rows, pixels), BF16),
             pltpu.VMEM((SIDE, group_rows, pixels), F32),
             pltpu.VMEM((8, pixels), F32),
@@ -527,7 +575,7 @@
             pltpu.VMEM((TILES, *TILE), F32),
             dma((SIDE,)), dma((SIDE,)), dma, dma, dma((SIDE,)), dma((SIDE,)), dma((SIDE,)), dma((SIDE,)), dma((SIDE,)), dma,
             dma((SIDE,)), dma((SIDE,)), dma((SIDE,)), dma((SIDE,)),
-            dma((SIDE,)), dma((SIDE,)), dma((SIDE,)), dma((SIDE,)), dma, dma,
+            dma((SIDE,)), dma((SIDE,)), dma((SIDE,)), dma((SIDE,)), dma((SIDE,)), dma((SIDE,)), dma, dma,
             dma((SIDE,)), dma((SIDE,)), dma, dma, dma, dma,
         ],
         compiler_params=pltpu.CompilerParams(

time: 58.9 us -> 62.6 us (1.063)
  Pallas kernels: 57.5 us -> 59.9 us
  local copies, waits for them, and re-layouts: 0 us -> 1.23 us
    pallas_call x1, Pallas kernels: 55.6 us -> 58.1 us  [on_device(): pl.pallas_call(lambda *refs: kernel(loss_scale, *refs), out_shape=(pltpu....]
    unnamed x0 -> x4, local copies, waits for them, and re-layouts: none -> 1.23 us
where the time goes in v6:
time: 62.6 us; the launch traced here: 61.8 us
  Pallas kernels  59.9 us (96%)
  local copies, waits for them, and re-layouts  1.23 us (2%)
  between operations  0.65 us (1%)
    pallas_call x1, Pallas kernels, on_device(): pl.pallas_call(lambda *refs: kernel(loss_scale, *refs), out_shape=(pltpu....  58.1 us
    pallas_call x1, Pallas kernels, on_device(): pl.pallas_call(results, out_shape=(jax.ShapeDtypeStruct((3, 1, pixels), F...  1.82 us

profile of v6, /device:TPU:1, one launch (start us, length us, event | category | flops | bytes accessed | tf_op | source)
XLA Modules:
  0.0 61.8 jit_solution(4896973281815585673)
XLA Ops:
  0.6 58.1 %shard_map.103 = (f32[3,1,1024]{2,1,0:T(1,128)S(1)}, f32[13,16,128]{2,1,0:T(8,128)S(1)}) custom-call(bf16[320,1024]{1,0:T(8,128)(2,1)} %bitcast.11, f32[64,320]{1,0:T(8,128)} %refs_1_.1, bf16[80,320]{1,0:T(8,128)(2,1)} %bitcast.14, bf16[80,320]{1,0:T(8,128)(2,1)} %bitcast.15, s32[1,64]{1,0:T(1,128)} %bitcast.18, f32[3,1,320]{2,1,0:T(1,128)} %bitcast.9, ...), custom_call_target="tpu_custom_call" | custom-call | flops 3019898880 | bytes 2097152 | tf_op jit(solution)/shard_map/pallas_call | solution.py:541
  58.7 0.0 copy-start
  58.7 0.6 %copy-done = f32[13,16,128]{2,1,0:T(8,128)} copy-done((f32[13,16,128]{2,1,0:T(8,128)}, f32[13,16,128]{2,1,0:T(8,128)S(1)}, u32[]{:S(2)}) %copy-start) | copy-done | bytes 106520
  59.3 0.0 copy-start.1
  59.3 0.6 copy-done.1
  59.9 1.8 %shard_map.104 = (f32[3,1,1024]{2,1,0:T(1,128)}, f32[80,320]{1,0:T(8,128)}, f32[80,320]{1,0:T(8,128)}) custom-call(f32[13,16,128]{2,1,0:T(8,128)} %copy-done, f32[3,1,1024]{2,1,0:T(1,128)} %copy-done.1, f32[3,1,320]{2,1,0:T(1,128)} %bitcast.10), custom_call_target="tpu_custom_call" | custom-call | tf_op jit(solution)/shard_map/pallas_call | solution.py:586
Async XLA Ops:
  58.7 0.6 %copy-start = (f32[13,16,128]{2,1,0:T(8,128)}, f32[13,16,128]{2,1,0:T(8,128)S(1)}, u32[]{:S(2)}) copy-start(f32[13,16,128]{2,1,0:T(8,128)S(1)} %get-tuple-element.8.sums_ref) | copy-start | bytes 319492
  59.3 0.6 copy-start.1

commit v7 on v5

--- a/solution.py
+++ b/solution.py
@@ -67,8 +67,11 @@
     pair = lax.axis_index("pair")
     dp = lax.axis_index("dp")
     fsdp = lax.axis_index("fsdp")
-    x, zl = dp // SIDE, dp % SIDE
-    y, zh = fsdp // SIDE, fsdp % SIDE
+    x, zl = lax.div(dp, SIDE), lax.rem(dp, SIDE)
+    y, zh = lax.div(fsdp, SIDE), lax.rem(fsdp, SIDE)
+    xs, ys, zls, zhs = ([at] + [lax.rem(at + n, SIDE) for n in range(1, SIDE)] for at in (x, y, zl, zh))
+    steps = (2, 1, 3, 0)
+    around = [(a, b) for b in steps for a in steps if (a, b) != (0, 0)]
     here = y * SIDE + x
     channels, pixels = x_ref.shape
     rows = w_in_ref.shape[0]
@@ -76,42 +79,33 @@
     def device(x_, y_, zh_, zl_):
         return (pair, x_ * SIDE + zl_, y_ * SIDE + zh_)
 
-    def plane_peer(i):
-        return device((x + i % SIDE) % SIDE, (y + i // SIDE) % SIDE, zh, zl)
-
-    def z_peer(i):
-        return device(x, y, (zh + i // SIDE) % SIDE, (zl + i % SIDE) % SIDE)
-
-    def dp_peer(i):
-        return device((x + i // SIDE) % SIDE, y, zh, (zl + i % SIDE) % SIDE)
+    def plane_peer(a, b):
+        return device(xs[a], ys[b], zh, zl)
+
+    def dp_peer(a, b):
+        return device(xs[a], y, zh, zls[b])
 
     def group_peer(k):
-        return device(x, y, (zh + k) % SIDE, zl)
-
+        return device(x, y, zhs[k], zl)
+
+    barrier = pltpu.get_barrier_semaphore()
+
+    def greet(peer):
+        pl.semaphore_signal(barrier, inc=1, device_id=peer, device_id_type=MESH)
+
+    for k in (1, 3):
+        greet(group_peer(k))
     loads = {}
     for n, (src, dst) in enumerate(
         ((w_in_hbm, w_in_ref), (w_down_hbm, w_down_ref), (x_hbm, x_ref), (table_hbm, table_ref))
     ):
         loads[n] = pltpu.make_async_copy(src, dst, in_sem.at[n])
         loads[n].start()
-
-    barrier = pltpu.get_barrier_semaphore()
-
-    def greet(peer):
-        pl.semaphore_signal(barrier, inc=1, device_id=peer, device_id_type=MESH)
-
-    def greet_all(i, carry):
-        greet(plane_peer(i))
-        return carry
-
-    lax.fori_loop(1, OTHERS + 1, greet_all, 0)
-    for a in range(SIDE):
-        for b in range(1, SIDE):
-            greet(dp_peer(a * SIDE + b))
-    for k in (1, 3):
-        greet(group_peer(k))
+    for a, b in around:
+        greet(plane_peer(a, b))
+        if b:
+            greet(dp_peer(a, b))
     greet((1 - pair, dp, fsdp))
-
     loads[0].wait()
     w_own = w_in_ref[...]
     last = w_own[:, 256:320].astype(F32)
@@ -145,7 +139,7 @@
     block = wbuf.at[zh, pl.ds(y * SIDE, SIDE)]
     along_y = []
     for m in range(1, SIDE):
-        c = remote(block, block, y_send.at[m], y_recv.at[m], device(x, (y + m) % SIDE, zh, zl))
+        c = remote(block, block, y_send.at[m], y_recv.at[m], plane_peer(0, m))
         c.start()
         along_y.append(c)
 
@@ -176,8 +170,7 @@
         along_z_ext[k] = remote(own_ext, own_ext, ax_send.at[k], ax_recv.at[k], group_peer(k))
         when_mine(zh, along_z_ext[k].start)
     for m in range(1, SIDE):
-        peer = device(x, (y + m) % SIDE, zh, zl)
-        c = remote(own_ext, own_ext, yx_send.at[m], yx_recv.at[m], peer)
+        c = remote(own_ext, own_ext, yx_send.at[m], yx_recv.at[m], plane_peer(0, m))
         c.start()
         along_y.append(c)
 
@@ -193,8 +186,9 @@
     gain = jnp.broadcast_to(gain, (128, 384)).T[:channels, 0:1]
     xf = x_ref[...].astype(F32)
     mean_sq = jnp.mean(xf * xf, axis=0, keepdims=True)
-    normed[0:channels, :] = (xf * lax.rsqrt(mean_sq + EPS) * gain).astype(BF16)
-    normed[channels:, :] = jnp.zeros((384 - channels, pixels), BF16)
+    whole = xf * lax.rsqrt(mean_sq + EPS) * gain
+    whole = jnp.concatenate([whole, jnp.zeros((384 - channels, pixels), F32)], axis=0)
+    normed[...] = whole.astype(BF16)
 
     row = lax.broadcasted_iota(jnp.int32, part.shape, 0)
     part = jnp.where(row < 3, part_hi, jnp.where(row < 6, part_mid, part_lo)).astype(BF16)
@@ -202,28 +196,34 @@
     pred_mine[...] = jnp.zeros_like(pred_mine)
     pred_mine[0:3, :] = direct[0:3] + direct[3:6] + direct[6:9]
 
-    wide = 256
+    wide = 512
+
+    def assemble(group, yy):
+        def tile(t):
+            return wbuf[group, yy * SIDE + t // SHARE, t % SHARE]
+
+        end = unpack_last(tile(10).astype(F32), tile(11).astype(F32), wext[group, yy].astype(F32))
+        for band in range(BANDS):
+            at = pl.ds(yy * rows + 16 * band, 16)
+            wmat[group, at, 0:128] = tile(band)
+            wmat[group, at, 128:256] = tile(BANDS + band)
+            wmat[group, at, 256:384] = end[band].astype(BF16)
+
+    def sigmoid(pre):
+        return 0.5 * jnp.tanh(0.5 * pre) + 0.5
 
     def forward(group, now=True):
-        def assemble(yy, carry):
-            def tile(t):
-                return wbuf[group, yy * SIDE + t // SHARE, t % SHARE]
-
-            end = unpack_last(tile(10).astype(F32), tile(11).astype(F32), wext[group, yy].astype(F32))
-            for band in range(BANDS):
-                at = pl.ds(yy * rows + 16 * band, 16)
-                wmat[group, at, 0:128] = tile(band)
-                wmat[group, at, 128:256] = tile(BANDS + band)
-                wmat[group, at, 256:384] = end[band].astype(BF16)
+        def assemble_one(yy, carry):
+            assemble(group, yy)
             return carry
 
-        lax.fori_loop(0, SIDE, assemble, 0)
+        lax.fori_loop(0, SIDE, assemble_one, 0)
         head_t[group] = wmat[group, :, 256:384].astype(F32).T[HEAD : HEAD + 16].astype(BF16)
 
         def columns(n, carry):
             at = pl.ds(pl.multiple_of(n * wide, wide), wide)
             pre = dot(wmat[group], normed[:, at], ((1,), (0,)))
-            sig = 0.5 * jnp.tanh(0.5 * pre) + 0.5
+            sig = sigmoid(pre)
             act = pre * sig
             hid = act.astype(BF16)
             hidden[group, :, at] = hid
@@ -234,32 +234,40 @@
 
         lax.fori_loop(0, pixels // wide, columns, 0, unroll=True)
 
+    relays = {}
+    passed = wext.at[zhs[1], y]
+    relay_ext = remote(passed, passed, ex_send, ex_recv, group_peer(3))
+
+    def relay(k):
+        group = zhs[-k]
+        along_z[k].wait_recv()
+        some = wbuf.at[group, here, pl.ds(0, 2) if k == 1 else pl.ds(2, 1)]
+        relays[k] = remote(some, some, e_send.at[k], e_recv.at[k], group_peer(k))
+        relays[k].start()
+        when_mine(group, along_z_ext[k].wait_recv)
+        if k == 3:
+            when_mine(group, relay_ext.start)
+
     def forward_on(k):
-        group = (zh + SIDE - k) % SIDE
+        group = zhs[-k]
         if k == 2:
             relays[1].wait_recv()
             relays[3].wait_recv()
             when_mine(group, relay_ext.wait_recv)
-        else:
-            along_z[k].wait_recv()
-            when_mine(group, along_z_ext[k].wait_recv)
-            some = wbuf.at[group, here, pl.ds(0, 2) if k == 1 else pl.ds(2, 1)]
-            relays[k] = remote(some, some, e_send.at[k], e_recv.at[k], group_peer(k))
-            relays[k].start()
-            if k == 3:
-                when_mine(group, relay_ext.start)
         chunk = wbuf.at[group, here]
         extra = wext.at[group, y]
 
-        def send(i, carry):
-            remote(chunk, chunk, b_send.at[k], b_recv.at[k], plane_peer(i)).start()
-            when_mine(group, remote(extra, extra, bx_send.at[k], bx_recv.at[k], plane_peer(i)).start)
-            return carry
-
-        lax.fori_loop(1, OTHERS + 1, send, 0)
-
+        for a, b in around:
+            remote(chunk, chunk, b_send.at[k], b_recv.at[k], plane_peer(a, b)).start()
+
+        @pl.when(x == group)
+        def _():
+            for a, b in around:
+                remote(extra, extra, bx_send.at[k], bx_recv.at[k], plane_peer(a, b)).start()
+
+    far = zhs[2]
     def wait_group(k):
-        group = (zh + SIDE - k) % SIDE
+        group = zhs[-k]
         wait_bytes(wbuf.at[0, 0:OTHERS], b_recv.at[k])
 
         @pl.when(x == group)
@@ -270,10 +278,8 @@
         def _():
             wait_bytes(wext.at[0], bx_recv.at[k])
 
-    relays = {}
-    passed = wext.at[(zh + 1) % SIDE, y]
-    relay_ext = remote(passed, passed, ex_send, ex_recv, group_peer(3))
     for k in (1, 3):
+        relay(k)
         forward_on(k)
     for c in along_y:
         c.wait_recv()
@@ -283,9 +289,11 @@
     weight = samples / (samples + 64.0)
     g_rows[...] = jnp.zeros_like(g_rows)
     g_aug[...] = jnp.zeros_like(g_aug)
-    for k in (1, 3, 2):
+    for k in (1, 3):
         wait_group(k)
-        forward((zh + SIDE - k) % SIDE, now=k != 2)
+        forward(zhs[-k])
+    wait_group(2)
+    forward(far, now=False)
 
     swap = remote(pred_mine, pred_other, p_send, p_recv, (1 - pair, dp, fsdp))
     swap.start()
@@ -294,12 +302,10 @@
         pred_ref[k] = pred[k : k + 1]
     toward = weight * (pred - target_ref[...])
 
-    far = (zh + 2) % SIDE
-
     def make_slope(n, carry):
         at = pl.ds(pl.multiple_of(n * wide, wide), wide)
         pre = slope[far, :, at]
-        sig = 0.5 * jnp.tanh(0.5 * pre) + 0.5
+        sig = sigmoid(pre)
         slope[far, :, at] = sig + pre * sig * (1.0 - sig)
         return carry
 
@@ -313,10 +319,10 @@
     g_aug[HEAD : HEAD + 16, :] = g_rows[...].astype(BF16)
 
     def backward_rows(group, picks):
-        ys = [(y + b) % SIDE for b in picks]
+        owners = [ys[b] for b in picks]
 
         def pick(ref, *rest):
-            return jnp.concatenate([ref[(group, pl.ds(yy * rows, rows), *rest)] for yy in ys], axis=0)
+            return jnp.concatenate([ref[(group, pl.ds(yy * rows, rows), *rest)] for yy in owners], axis=0)
 
         g_hidden = dot(pick(wmat, slice(256, 384)), g_aug[...], ((1,), (0,)))
         g_pre = (g_hidden * pick(slope, slice(None))).astype(BF16)
@@ -325,50 +331,44 @@
         lane_g = lax.broadcasted_iota(jnp.int32, for_head.shape, 1)
         is_rest = (lane_g >= HEAD + 3) & (lane_g < HEAD + 6)
         for_head = jnp.where(is_rest, for_head - for_head.astype(BF16).astype(F32), for_head)
-        for n, yy in enumerate(ys):
+        for n, yy in enumerate(owners):
             at = slice(n * rows, n * rows + rows)
             tiles = pack(grad[at, 0:128], grad[at, 128:256], grad[at, 256:384])
             for t in range(TILES - 1):
                 gsend[group, yy * SIDE + t // SHARE, t % SHARE] = tiles[t]
             gext[group, yy] = pack_end(grad[at, 256:384], for_head[at])
 
-        for b in picks:
-            yy = (y + b) % SIDE
-
-            def send(a, carry):
-                xx = (x + a) % SIDE
+        for a, b in around:
+            if b in picks:
                 remote(
-                    gsend.at[group, yy * SIDE + xx], grecv.at[group, here],
-                    r_send.at[group], r_recv.at[group], device(xx, yy, zh, zl),
+                    gsend.at[group, ys[b] * SIDE + xs[a]], grecv.at[group, here],
+                    r_send.at[group], r_recv.at[group], plane_peer(a, b),
                 ).start()
-                return carry
-
-            lax.fori_loop(1 if b == 0 else 0, SIDE, send, 0)
 
     def backward(group, parts):
         for picks in parts:
             backward_rows(group, picks)
         grecv[group, here] = gsend[group, here]
 
-        def send_ext(b, carry):
-            to = (y + b) % SIDE
+        def send_ext(b):
             remote(
-                gext.at[group, to], xrecv.at[here], rx_send.at[group], rx_recv, device(group, to, zh, zl)
+                gext.at[group, ys[b]], xrecv.at[here], rx_send.at[group], rx_recv, device(group, ys[b], zh, zl)
             ).start()
-            return carry
+
+        for b in (2, 1, 3):
+            send_ext(b)
 
         @pl.when(x == group)
         def _():
-            lax.fori_loop(1, SIDE, send_ext, 0)
             xrecv[here] = gext[group, y]
 
         @pl.when(x != group)
         def _():
-            lax.fori_loop(0, SIDE, send_ext, 0)
-
-    order = [(zh + k) % SIDE for k in (2, 1, 3, 0)]
-
-    def plane_sum(group):
+            send_ext(0)
+
+    order = [zhs[k] for k in steps]
+
+    def plane_sum(group, own):
         wait_bytes(grecv.at[0, 0:OTHERS], r_recv.at[group])
         total = grecv[group, 0].astype(F32)
         for s in range(1, SIDE * SIDE):
@@ -377,14 +377,12 @@
 
         own_slot = zrecv.at[zh * SIDE + zl]
 
-        def send(to, carry):
-            @pl.when((group != zh) | (to != zl))
-            def _():
-                remote(zsend.at[group, to], own_slot, z_send, z_recv, device(x, y, group, to)).start()
-
-            return carry
-
-        lax.fori_loop(0, SHARE, send, 0)
+        for to in range(SHARE):
+            piece = remote(zsend.at[group, to], own_slot, z_send, z_recv, device(x, y, group, to))
+            if own:
+                pl.when(to != zl)(piece.start)
+            else:
+                piece.start()
 
         @pl.when(x == group)
         def _():
@@ -394,15 +392,16 @@
                 total = total + xrecv[s].astype(F32)
             zext[...] = total
 
-            @pl.when((group != zh) | (zl != SHARE))
-            def _():
-                remote(zext, own_slot, z_send, z_recv, device(x, y, group, SHARE)).start()
-
-    whole = (2, 1, 3, 0)
+            piece = remote(zext, own_slot, z_send, z_recv, device(x, y, group, SHARE))
+            if own:
+                pl.when(zl != SHARE)(piece.start)
+            else:
+                piece.start()
+
     for n, group in enumerate(order):
-        backward(group, (whole[:2], whole[2:]) if n == 0 else (whole,))
-    for group in order:
-        plane_sum(group)
+        backward(group, ((2, 1), (3, 0)) if n == 0 else ((2, 1, 3, 0),))
+    for k, group in zip(steps, order):
+        plane_sum(group, k == 0)
     has_tile = (zl < SHARE) | (x == zh)
 
     @pl.when(zl < SHARE)
@@ -422,21 +421,18 @@
         own = jnp.where(zl < SHARE, x * SHARE + zl, TILES - 1)
         fbuf[own] = total
 
-        def send_piece(i, carry):
-            remote(fbuf.at[own], fbuf.at[own], f_send, f_recv, dp_peer(i)).start()
-            return carry
-
-        lax.fori_loop(1, OTHERS + 1, send_piece, 0)
+        for a, b in around:
+            remote(fbuf.at[own], fbuf.at[own], f_send, f_recv, dp_peer(a, b)).start()
 
     for k in (1, 2, 3):
-        group = (zh + SIDE - k) % SIDE
+        group = zhs[-k]
         if k != 2:
             along_z[k].wait_send()
             when_mine(zh, along_z_ext[k].wait_send)
             relays[k].wait_send()
         wait_bytes(wbuf.at[0, 0:OTHERS], b_send.at[k])
         when_mine(group, lambda: wait_bytes(xrecv.at[0:OTHERS], bx_send.at[k]))
-    when_mine((zh + 1) % SIDE, relay_ext.wait_send)
+    when_mine(zhs[1], relay_ext.wait_send)
     for c in along_y:
         c.wait_send()
     swap.wait_send()

time: 58.9 us -> 57.7 us (0.980)
  Pallas kernels: 57.5 us -> 56.8 us
    pallas_call x1, Pallas kernels: 55.6 us -> 55 us  [on_device(): pl.pallas_call(lambda *refs: kernel(loss_scale, *refs), out_shape=(jax.Sh...]
where the time goes in v7:
time: 57.7 us; the launch traced here: 57.4 us
  Pallas kernels  56.8 us (98%)
  between operations  0.64 us (1%)
    pallas_call x1, Pallas kernels, on_device(): pl.pallas_call(lambda *refs: kernel(loss_scale, *refs), out_shape=(jax.Sh...  55 us
    pallas_call x1, Pallas kernels, on_device(): pl.pallas_call(results, out_shape=(jax.ShapeDtypeStruct((3, 1, pixels), F...  1.82 us

profile of v7, /device:TPU:1, one launch (start us, length us, event | category | flops | bytes accessed | tf_op | source)
XLA Modules:
  0.0 57.4 jit_solution(14722536328714209685)
XLA Ops:
  0.6 55.0 %shard_map.103 = (f32[3,1,1024]{2,1,0:T(1,128)}, f32[13,16,128]{2,1,0:T(8,128)}) custom-call(bf16[320,1024]{1,0:T(8,128)(2,1)} %bitcast.11, f32[64,320]{1,0:T(8,128)} %refs_1_.1, bf16[80,320]{1,0:T(8,128)(2,1)} %bitcast.14, bf16[80,320]{1,0:T(8,128)(2,1)} %bitcast.15, s32[1,64]{1,0:T(1,128)} %bitcast.18, f32[3,1,320]{2,1,0:T(1,128)} %bitcast.9, ...), custom_call_target="tpu_custom_call" | custom-call | flops 3019898880 | bytes 2097152 | tf_op jit(solution)/shard_map/pallas_call | solution.py:489
  55.6 1.8 %shard_map.104 = (f32[3,1,1024]{2,1,0:T(1,128)}, f32[80,320]{1,0:T(8,128)}, f32[80,320]{1,0:T(8,128)}) custom-call(f32[13,16,128]{2,1,0:T(8,128)} %get-tuple-element.8.sums_ref, f32[3,1,1024]{2,1,0:T(1,128)} %get-tuple-element.9.pred_in_ref, f32[3,1,320]{2,1,0:T(1,128)} %bitcast.10), custom_call_target="tpu_custom_call" | custom-call | tf_op jit(solution)/shard_map/pallas_call | solution.py:534

commit v8 on v7

--- a/solution.py
+++ b/solution.py
@@ -36,7 +36,7 @@
 
 def pack_end(last, head):
     band = [slice(16 * b, 16 * b + 16) for b in range(BANDS)]
-    end = last[band[4]] + head[band[0]]
+    end = last + head[band[0]]
     for b in range(1, BANDS):
         end = end + pltpu.roll(head[band[b]], PARTS * b, 1)
     return end.astype(BF16)
@@ -58,7 +58,7 @@
     x_hbm, table_hbm, w_in_hbm, w_down_hbm, levels_ref, w_rgb_ref, target_ref, counts_ref,
     pred_ref, sums_ref,
     x_ref, table_ref, w_in_ref, w_down_ref, in_sem,
-    rgb_rows, rgb_parts, normed, wbuf, wext, wmat, head_t, hidden, slope, pred_mine, pred_other, g_rows, g_aug,
+    rgb_rows, rgb_parts, normed, wbuf, wext, wmat, head_t, hidden, slope, pred_mine, pred_other, g_rows, g_aug, g_aug_t, ends,
     gsend, gext, grecv, xrecv, zsend, zext, zrecv, fbuf,
     ax_send, ax_recv, ex_send, ex_recv, yx_send, yx_recv, bx_send, bx_recv, rx_send, rx_recv,
     a_send, a_recv, e_send, e_recv, y_send, y_recv, b_send, b_recv, p_send, p_recv,
@@ -103,8 +103,8 @@
         loads[n].start()
     for a, b in around:
         greet(plane_peer(a, b))
-        if b:
-            greet(dp_peer(a, b))
+    for b in (2, 1, 3):
+        greet(dp_peer(0, b))
     greet((1 - pair, dp, fsdp))
     loads[0].wait()
     w_own = w_in_ref[...]
@@ -113,35 +113,6 @@
     tiles = pack(w_own[:, 0:128], w_own[:, 128:256], last)
     for t in range(TILES - 1):
         wbuf[zh, y * SIDE + t // SHARE, t % SHARE] = tiles[t]
-
-    pl.semaphore_wait(barrier, OTHERS + 12 + 2 + 1)
-
-    def remote(src, dst, send, recv, peer):
-        return pltpu.make_async_remote_copy(
-            src_ref=src, dst_ref=dst, send_sem=send, recv_sem=recv,
-            device_id=peer, device_id_type=MESH,
-        )
-
-    def wait_bytes(ref, sem):
-        pltpu.make_async_copy(ref, ref, sem).wait()
-
-    quarter = wbuf.at[zh, here]
-    along_z = {}
-    for k in (1, 3):
-        along_z[k] = remote(quarter, quarter, a_send.at[k], a_recv.at[k], group_peer(k))
-        along_z[k].start()
-
-    def when_mine(group, copy):
-        @pl.when(x == group)
-        def _():
-            copy()
-
-    block = wbuf.at[zh, pl.ds(y * SIDE, SIDE)]
-    along_y = []
-    for m in range(1, SIDE):
-        c = remote(block, block, y_send.at[m], y_recv.at[m], plane_peer(0, m))
-        c.start()
-        along_y.append(c)
 
     rgb_rows[...] = jnp.zeros_like(rgb_rows)
     for copy in range(3):
@@ -164,7 +135,36 @@
     is_lo = (lane >= HEAD + 3) & (lane < HEAD + 6)
     head = jnp.where(is_lo, head - head_hi, head_hi)
     own_ext = wext.at[zh, y]
-    own_ext[...] = pack_end(last, head)
+    own_ext[...] = pack_end(last[64:80], head)
+    pl.semaphore_wait(barrier, OTHERS + 3 + 2 + 1)
+
+    def remote(src, dst, send, recv, peer):
+        return pltpu.make_async_remote_copy(
+            src_ref=src, dst_ref=dst, send_sem=send, recv_sem=recv,
+            device_id=peer, device_id_type=MESH,
+        )
+
+    def wait_bytes(ref, sem):
+        pltpu.make_async_copy(ref, ref, sem).wait()
+
+    quarter = wbuf.at[zh, here]
+    along_z = {}
+    for k in (1, 3):
+        along_z[k] = remote(quarter, quarter, a_send.at[k], a_recv.at[k], group_peer(k))
+        along_z[k].start()
+
+    def when_mine(group, copy):
+        @pl.when(x == group)
+        def _():
+            copy()
+
+    block = wbuf.at[zh, pl.ds(y * SIDE, SIDE)]
+    along_y = []
+    for m in range(1, SIDE):
+        c = remote(block, block, y_send.at[m], y_recv.at[m], plane_peer(0, m))
+        c.start()
+        along_y.append(c)
+
     along_z_ext = {}
     for k in (1, 3):
         along_z_ext[k] = remote(own_ext, own_ext, ax_send.at[k], ax_recv.at[k], group_peer(k))
@@ -244,16 +244,12 @@
         some = wbuf.at[group, here, pl.ds(0, 2) if k == 1 else pl.ds(2, 1)]
         relays[k] = remote(some, some, e_send.at[k], e_recv.at[k], group_peer(k))
         relays[k].start()
-        when_mine(group, along_z_ext[k].wait_recv)
-        if k == 3:
-            when_mine(group, relay_ext.start)
 
     def forward_on(k):
         group = zhs[-k]
         if k == 2:
             relays[1].wait_recv()
             relays[3].wait_recv()
-            when_mine(group, relay_ext.wait_recv)
         chunk = wbuf.at[group, here]
         extra = wext.at[group, y]
 
@@ -262,6 +258,12 @@
 
         @pl.when(x == group)
         def _():
+            if k == 2:
+                relay_ext.wait_recv()
+            else:
+                along_z_ext[k].wait_recv()
+            if k == 3:
+                relay_ext.start()
             for a, b in around:
                 remote(extra, extra, bx_send.at[k], bx_recv.at[k], plane_peer(a, b)).start()
 
@@ -327,16 +329,12 @@
         g_hidden = dot(pick(wmat, slice(256, 384)), g_aug[...], ((1,), (0,)))
         g_pre = (g_hidden * pick(slope, slice(None))).astype(BF16)
         grad = dot(g_pre, normed[...], ((1,), (1,)))
-        for_head = dot(pick(hidden, slice(None)), g_aug[...], ((1,), (1,)))
-        lane_g = lax.broadcasted_iota(jnp.int32, for_head.shape, 1)
-        is_rest = (lane_g >= HEAD + 3) & (lane_g < HEAD + 6)
-        for_head = jnp.where(is_rest, for_head - for_head.astype(BF16).astype(F32), for_head)
         for n, yy in enumerate(owners):
             at = slice(n * rows, n * rows + rows)
             tiles = pack(grad[at, 0:128], grad[at, 128:256], grad[at, 256:384])
             for t in range(TILES - 1):
                 gsend[group, yy * SIDE + t // SHARE, t % SHARE] = tiles[t]
-            gext[group, yy] = pack_end(grad[at, 256:384], for_head[at])
+            ends[yy] = grad[n * rows + 64 : n * rows + 80, 256:384]
 
         for a, b in around:
             if b in picks:
@@ -345,10 +343,19 @@
                     r_send.at[group], r_recv.at[group], plane_peer(a, b),
                 ).start()
 
-    def backward(group, parts):
+    def backward(group, parts, first):
         for picks in parts:
             backward_rows(group, picks)
         grecv[group, here] = gsend[group, here]
+
+        if first:
+            g_aug_t[...] = g_aug[...].astype(F32).T.astype(BF16)
+        for_head = dot(hidden[group], g_aug_t[...], ((1,), (0,)))
+        lane_g = lax.broadcasted_iota(jnp.int32, for_head.shape, 1)
+        is_rest = (lane_g >= HEAD + 3) & (lane_g < HEAD + 6)
+        for_head = jnp.where(is_rest, for_head - for_head.astype(BF16).astype(F32), for_head)
+        for yy in range(SIDE):
+            gext[group, yy] = pack_end(ends[yy], for_head[yy * rows : yy * rows + rows])
 
         def send_ext(b):
             remote(
@@ -399,7 +406,7 @@
                 piece.start()
 
     for n, group in enumerate(order):
-        backward(group, ((2, 1), (3, 0)) if n == 0 else ((2, 1, 3, 0),))
+        backward(group, ((2, 1), (3, 0)) if n == 0 else ((2, 1, 3, 0),), n == 0)
     for k, group in zip(steps, order):
         plane_sum(group, k == 0)
     has_tile = (zl < SHARE) | (x == zh)
@@ -513,6 +520,8 @@
             pltpu.VMEM((8, pixels), F32),
             pltpu.VMEM((16, pixels), F32),
             pltpu.VMEM((128, pixels), BF16),
+            pltpu.VMEM((pixels, 128), BF16),
+            pltpu.VMEM((SIDE, *TILE), F32),
             pltpu.VMEM((SIDE, plane, SHARE, *TILE), BF16),
             pltpu.VMEM((SIDE, SIDE, *TILE), BF16),
             pltpu.VMEM((SIDE, plane, SHARE, *TILE), BF16),

time: 57.7 us -> 57.3 us (level)
  Pallas kernels: 56.8 us -> 56.1 us
    pallas_call x1, Pallas kernels: 55 us -> 54.3 us  [on_device(): pl.pallas_call(lambda *refs: kernel(loss_scale, *refs), out_shape=(jax.Sh...]
where the time goes in v8:
time: 57.3 us; the launch traced here: 56.8 us
  Pallas kernels  56.1 us (98%)
  between operations  0.64 us (1%)
    pallas_call x1, Pallas kernels, on_device(): pl.pallas_call(lambda *refs: kernel(loss_scale, *refs), out_shape=(jax.Sh...  54.3 us
    pallas_call x1, Pallas kernels, on_device(): pl.pallas_call(results, out_shape=(jax.ShapeDtypeStruct((3, 1, pixels), F...  1.82 us

profile of v8, /device:TPU:1, one launch (start us, length us, event | category | flops | bytes accessed | tf_op | source)
XLA Modules:
  0.0 56.8 jit_solution(4129481010035380762)
XLA Ops:
  0.6 54.3 %shard_map.103 = (f32[3,1,1024]{2,1,0:T(1,128)}, f32[13,16,128]{2,1,0:T(8,128)}) custom-call(bf16[320,1024]{1,0:T(8,128)(2,1)} %bitcast.11, f32[64,320]{1,0:T(8,128)} %refs_1_.1, bf16[80,320]{1,0:T(8,128)(2,1)} %bitcast.14, bf16[80,320]{1,0:T(8,128)(2,1)} %bitcast.15, s32[1,64]{1,0:T(1,128)} %bitcast.18, f32[3,1,320]{2,1,0:T(1,128)} %bitcast.9, ...), custom_call_target="tpu_custom_call" | custom-call | flops 3019898880 | bytes 2097152 | tf_op jit(solution)/shard_map/pallas_call | solution.py:496
  54.9 1.8 %shard_map.104 = (f32[3,1,1024]{2,1,0:T(1,128)}, f32[80,320]{1,0:T(8,128)}, f32[80,320]{1,0:T(8,128)}) custom-call(f32[13,16,128]{2,1,0:T(8,128)} %get-tuple-element.8.sums_ref, f32[3,1,1024]{2,1,0:T(1,128)} %get-tuple-element.9.pred_in_ref, f32[3,1,320]{2,1,0:T(1,128)} %bitcast.10), custom_call_target="tpu_custom_call" | custom-call | tf_op jit(solution)/shard_map/pallas_call | solution.py:543

commit v9 on v8

--- a/solution.py
+++ b/solution.py
@@ -196,7 +196,7 @@
     pred_mine[...] = jnp.zeros_like(pred_mine)
     pred_mine[0:3, :] = direct[0:3] + direct[3:6] + direct[6:9]
 
-    wide = 512
+    wide = 1024
 
     def assemble(group, yy):
         def tile(t):
@@ -406,7 +406,7 @@
                 piece.start()
 
     for n, group in enumerate(order):
-        backward(group, ((2, 1), (3, 0)) if n == 0 else ((2, 1, 3, 0),), n == 0)
+        backward(group, ((2, 1, 3, 0),), n == 0)
     for k, group in zip(steps, order):
         plane_sum(group, k == 0)
     has_tile = (zl < SHARE) | (x == zh)

time: 57.3 us -> 57.1 us (level)
  no operation moved by 1% of the time
where the time goes in v9:
time: 57.1 us; the launch traced here: 56.7 us
  Pallas kernels  56.1 us (98%)
  between operations  0.64 us (1%)
    pallas_call x1, Pallas kernels, on_device(): pl.pallas_call(lambda *refs: kernel(loss_scale, *refs), out_shape=(jax.Sh...  54.2 us
    pallas_call x1, Pallas kernels, on_device(): pl.pallas_call(results, out_shape=(jax.ShapeDtypeStruct((3, 1, pixels), F...  1.82 us

profile of v9, /device:TPU:1, one launch (start us, length us, event | category | flops | bytes accessed | tf_op | source)
XLA Modules:
  0.0 56.7 jit_solution(15973991959603599137)
XLA Ops:
  0.6 54.2 %shard_map.103 = (f32[3,1,1024]{2,1,0:T(1,128)}, f32[13,16,128]{2,1,0:T(8,128)}) custom-call(bf16[320,1024]{1,0:T(8,128)(2,1)} %bitcast.11, f32[64,320]{1,0:T(8,128)} %refs_1_.1, bf16[80,320]{1,0:T(8,128)(2,1)} %bitcast.14, bf16[80,320]{1,0:T(8,128)(2,1)} %bitcast.15, s32[1,64]{1,0:T(1,128)} %bitcast.18, f32[3,1,320]{2,1,0:T(1,128)} %bitcast.9, ...), custom_call_target="tpu_custom_call" | custom-call | flops 3019898880 | bytes 2097152 | tf_op jit(solution)/shard_map/pallas_call | solution.py:496
  54.9 1.8 %shard_map.104 = (f32[3,1,1024]{2,1,0:T(1,128)}, f32[80,320]{1,0:T(8,128)}, f32[80,320]{1,0:T(8,128)}) custom-call(f32[13,16,128]{2,1,0:T(8,128)} %get-tuple-element.8.sums_ref, f32[3,1,1024]{2,1,0:T(1,128)} %get-tuple-element.9.pred_in_ref, f32[3,1,320]{2,1,0:T(1,128)} %bitcast.10), custom_call_target="tpu_custom_call" | custom-call | tf_op jit(solution)/shard_map/pallas_call | solution.py:543
